TPU v7x, 256 devices: a whole 4x4x8 slice. The times are simulated.
256 devices in a mesh: resp: 32 (over y_hi, z, core), head: 8 (over y_lo, x).
Axes of the slice: x: 4, y: 4 (y_hi: 2, y_lo: 2; y = y_hi * 2 + y_lo), z: 8, core: 2. Of those that a mesh axis runs over, the one named last changes fastest.
Arguments:
- upper_input: bfloat16 [2048, 5120], P('resp', 'head'), may hold values from -100 to 100
- upper_gain: bfloat16 [5120], P('head'), may hold values from 0.099609375 to 1.8984375
- upper_key_weight: bfloat16 [5120, 1024], P(None, 'head'), may hold values from -0.1875 to 0.1875
- upper_value_weight: bfloat16 [5120, 1024], P(None, 'head'), may hold values from -0.1875 to 0.1875
- upper_prompt_keys: bfloat16 [2048, 1024], P(None, 'head'), may hold values from -4.5 to 4.5
- upper_prompt_values: bfloat16 [2048, 1024], P(None, 'head'), may hold values from -6 to 6
- upper_queries: bfloat16 [4096, 8192], P('resp', 'head'), may hold values from -120 to 120
- upper_span_keys: bfloat16 [4096, 1024], P('resp', 'head'), may hold values from -16 to 16
- upper_span_values: bfloat16 [4096, 1024], P('resp', 'head'), may hold values from -6 to 6
- upper_out_grad: bfloat16 [4096, 8192], P('resp', 'head'), may hold values from -96 to 96
- lower_input: bfloat16 [2048, 5120], P('resp', 'head'), may hold values from -100 to 100
- lower_gain: bfloat16 [5120], P('head'), may hold values from 0.099609375 to 1.8984375
- lower_key_weight: bfloat16 [5120, 1024], P(None, 'head'), may hold values from -0.1875 to 0.1875
- lower_value_weight: bfloat16 [5120, 1024], P(None, 'head'), may hold values from -0.1875 to 0.1875
- lower_prompt_keys: bfloat16 [2048, 1024], P(None, 'head'), may hold values from -4.5 to 4.5
- lower_prompt_values: bfloat16 [2048, 1024], P(None, 'head'), may hold values from -6 to 6
- lower_queries: bfloat16 [4096, 8192], P('resp', 'head'), may hold values from -120 to 120
- lower_span_keys: bfloat16 [4096, 1024], P('resp', 'head'), may hold values from -16 to 16
- lower_span_values: bfloat16 [4096, 1024], P('resp', 'head'), may hold values from -6 to 6
- lower_out_grad: bfloat16 [4096, 8192], P('resp', 'head'), may hold values from -96 to 96
Outputs:
- upper_query_grads: bfloat16 [4096, 8192], P('resp', 'head')
- lower_query_grads: bfloat16 [4096, 8192], P('resp', 'head')
- upper_span_grads: bfloat16 [4096, 2048], P('resp', 'head')
- lower_span_grads: bfloat16 [4096, 2048], P('resp', 'head')
- prompt_grads: bfloat16 [2048, 5120], P('resp', 'head')
All inputs are finite; a program needn't handle non-finite values.
Results may differ from a plain program's by a relative error of at most 0.02.
Values may be sent and summed in bfloat16 or wider, within the bound.
No kernel may reach another device: no remote copies, remote signals or barrier semaphores. Data moves between devices by JAX's collectives and lax.ppermute only.
A program may use at most 128 MiB of HBM per device.

v0:
```python
import jax
import jax.numpy as jnp
from jax import lax
from jax.sharding import PartitionSpec as P

D = 5120
C = 64


epsilon = 1e-06
masked = -1e30


def attend(queries, prompt_keys, prompt_values, span_keys, span_values, out_grad):
    tokens = queries.shape[0]
    head_size = span_keys.shape[1]
    groups = queries.shape[1] // head_size
    prompt = prompt_keys.shape[0]
    scale = head_size ** (-0.5)
    query_rows = queries.reshape(tokens, groups, head_size)
    grad_rows = out_grad.reshape(tokens, groups, head_size)
    positions = jnp.arange(tokens)
    causal = (positions[:, None] // C == positions[None, :] // C) & (
        positions[None, :] <= positions[:, None]
    )
    span_scores = (
        jnp.einsum("tgd,sd->gts", query_rows, span_keys, preferred_element_type=jnp.float32) * scale
    )
    span_scores = jnp.where(causal[None], span_scores, masked)
    block = min(512, prompt)
    count = prompt // block
    key_blocks = prompt_keys.reshape(count, block, head_size)
    value_blocks = prompt_values.reshape(count, block, head_size)

    def scores(key_block):
        return (
            jnp.einsum("tgd,jd->gtj", query_rows, key_block, preferred_element_type=jnp.float32)
            * scale
        )

    def running(carry, key_block):
        highest, total = carry
        block_scores = scores(key_block)
        new_highest = jnp.maximum(highest, jnp.max(block_scores, axis=2))
        total = total * jnp.exp(highest - new_highest) + jnp.sum(
            jnp.exp(block_scores - new_highest[..., None]), axis=2
        )
        return ((new_highest, total), None)

    highest = jnp.max(span_scores, axis=2)
    total = jnp.sum(jnp.exp(span_scores - highest[..., None]), axis=2)
    (highest, total), unused = lax.scan(running, (highest, total), key_blocks)

    def weights_of(block_scores):
        return jnp.exp(block_scores - highest[..., None]) / total[..., None]

    span_weights = weights_of(span_scores)
    span_dots = jnp.einsum(
        "tgd,sd->gts", grad_rows, span_values, preferred_element_type=jnp.float32
    )
    delta = jnp.sum(span_weights * span_dots, axis=2)

    def accumulate(carry, items):
        block_weights = weights_of(scores(items[0]))
        block_dots = jnp.einsum(
            "tgd,jd->gtj", grad_rows, items[1], preferred_element_type=jnp.float32
        )
        return (carry + jnp.sum(block_weights * block_dots, axis=2), None)

    delta, unused = lax.scan(accumulate, delta, (key_blocks, value_blocks))

    def backward(carry, items):
        block_weights = weights_of(scores(items[0]))
        block_dots = jnp.einsum(
            "tgd,jd->gtj", grad_rows, items[1], preferred_element_type=jnp.float32
        )
        slopes = (block_weights * (block_dots - delta[..., None])).astype(jnp.bfloat16)
        rounded_weights = block_weights.astype(jnp.bfloat16)
        carry = carry + jnp.einsum(
            "gtj,jd->tgd", slopes, items[0], preferred_element_type=jnp.float32
        )
        key_grad = (
            jnp.einsum("gtj,tgd->jd", slopes, query_rows, preferred_element_type=jnp.float32)
            * scale
        )
        value_grad = jnp.einsum(
            "gtj,tgd->jd", rounded_weights, grad_rows, preferred_element_type=jnp.float32
        )
        return (carry, jnp.concatenate([key_grad, value_grad], axis=1))

    span_slopes = (span_weights * (span_dots - delta[..., None])).astype(jnp.bfloat16)
    query_sums = jnp.einsum(
        "gts,sd->tgd", span_slopes, span_keys, preferred_element_type=jnp.float32
    )
    query_sums, prompt_terms = lax.scan(backward, query_sums, (key_blocks, value_blocks))
    query_grads = (query_sums * scale).astype(jnp.bfloat16).reshape(tokens, groups * head_size)
    span_key_grads = (
        jnp.einsum("gts,tgd->sd", span_slopes, query_rows, preferred_element_type=jnp.float32)
        * scale
    )
    span_value_grads = jnp.einsum(
        "gts,tgd->sd",
        span_weights.astype(jnp.bfloat16),
        grad_rows,
        preferred_element_type=jnp.float32,
    )
    span_grads = jnp.concatenate([span_key_grads, span_value_grads], axis=1).astype(jnp.bfloat16)
    return (query_grads, span_grads, prompt_terms.reshape(prompt, 2 * head_size))


def hidden_grad(summed_rows, key_weight, value_weight, hidden, norm_gain, inverse):
    rounded_rows = summed_rows.astype(jnp.bfloat16)
    head_size = summed_rows.shape[1] // 2
    key_rows = rounded_rows[:, :head_size]
    value_rows = rounded_rows[:, head_size:]
    contract = (((1,), (1,)), ((), ()))
    local_terms = lax.dot_general(
        key_rows, key_weight, contract, preferred_element_type=jnp.float32
    )
    local_terms = local_terms + lax.dot_general(
        value_rows, value_weight, contract, preferred_element_type=jnp.float32
    )
    projected = lax.psum_scatter(
        local_terms.astype(jnp.bfloat16), "head", scatter_dimension=1, tiled=True
    ).astype(jnp.float32)
    scaled = norm_gain.astype(jnp.float32)[None, :] * projected
    row_sums = lax.psum(jnp.sum(scaled * hidden, axis=1), "head")
    return inverse[:, None] * scaled - hidden * (inverse**3)[:, None] * row_sums[:, None] / D


def body(
    upper_input,
    upper_gain,
    upper_key_weight,
    upper_value_weight,
    upper_prompt_keys,
    upper_prompt_values,
    upper_queries,
    upper_span_keys,
    upper_span_values,
    upper_out_grad,
    lower_input,
    lower_gain,
    lower_key_weight,
    lower_value_weight,
    lower_prompt_keys,
    lower_prompt_values,
    lower_queries,
    lower_span_keys,
    lower_span_values,
    lower_out_grad,
):
    upper_hidden = upper_input.astype(jnp.float32)
    lower_hidden = lower_input.astype(jnp.float32)
    squares = lax.psum(
        (
            jnp.sum(upper_hidden * upper_hidden, axis=1),
            jnp.sum(lower_hidden * lower_hidden, axis=1),
        ),
        "head",
    )
    upper_inverse = lax.rsqrt(squares[0] / D + epsilon)
    lower_inverse = lax.rsqrt(squares[1] / D + epsilon)
    upper_query, upper_span, upper_terms = attend(
        upper_queries,
        upper_prompt_keys,
        upper_prompt_values,
        upper_span_keys,
        upper_span_values,
        upper_out_grad,
    )
    lower_query, lower_span, lower_terms = attend(
        lower_queries,
        lower_prompt_keys,
        lower_prompt_values,
        lower_span_keys,
        lower_span_values,
        lower_out_grad,
    )
    joined = jnp.concatenate([upper_terms, lower_terms], axis=1)
    width = upper_terms.shape[1]
    both_rows = lax.psum_scatter(joined, "resp", scatter_dimension=0, tiled=True)
    upper_rows = both_rows[:, :width]
    lower_rows = both_rows[:, width:]
    upper_grad = hidden_grad(
        upper_rows, upper_key_weight, upper_value_weight, upper_hidden, upper_gain, upper_inverse
    )
    lower_grad = hidden_grad(
        lower_rows, lower_key_weight, lower_value_weight, lower_hidden, lower_gain, lower_inverse
    )
    prompt_grads = (upper_grad + lower_grad).astype(jnp.bfloat16)
    return (upper_query, lower_query, upper_span, lower_span, prompt_grads)


def solution(mesh):
    placed = (
        P("resp", "head"),
        P("head"),
        P(None, "head"),
        P(None, "head"),
        P(None, "head"),
        P(None, "head"),
        P("resp", "head"),
        P("resp", "head"),
        P("resp", "head"),
        P("resp", "head"),
        P("resp", "head"),
        P("head"),
        P(None, "head"),
        P(None, "head"),
        P(None, "head"),
        P(None, "head"),
        P("resp", "head"),
        P("resp", "head"),
        P("resp", "head"),
        P("resp", "head"),
    )
    return jax.shard_map(
        body,
        mesh=mesh,
        in_specs=placed,
        out_specs=(
            P("resp", "head"),
            P("resp", "head"),
            P("resp", "head"),
            P("resp", "head"),
            P("resp", "head"),
        ),
        check_vma=False,
    )
```

profile of v0, /device:TPU:2, one launch (start us, length us, event | category | flops | bytes accessed | tf_op | source)
XLA Modules:
  0.0 373.8 jit_solution(8482248161299018137)
XLA Ops:
  7.4 1.9 copy.115
  16.7 7.2 %while.71 = (s32[]{:T(128)}, f32[8,128]{1,0:T(8,128)S(1)}, f32[8,128]{1,0:T(8,128)S(1)}, bf16[4,512,128]{2,1,0:T(8,128)(2,1)}, bf16[128,8,128]{2,0,1:T(8,128)(2,1)S(1)}, /*index=5*/s32[]{:T(128)}) while((s32[]{:T(128)}, f32[8,128]{1,0:T(8,128)S(1)}, f32[8,128]{1,0:T(8,128)S(1)}, bf16[4,512,128]{2,1,0:T(8,128)(2,1)}, ...), condition=%wide.region_17.18_spmd, body=%wide.region_14.17_spmd.sunk | while | flops 136841216 | bytes 4640849 | solution.py:52
  25.2 7.2 %while.68 = (s32[]{:T(128)}, f32[8,128]{1,0:T(8,128)S(1)}, f32[8,128]{1,0:T(8,128)S(1)}, bf16[4,512,128]{2,1,0:T(8,128)(2,1)}, bf16[128,8,128]{2,0,1:T(8,128)(2,1)S(1)}, /*index=5*/s32[]{:T(128)}) while((s32[]{:T(128)}, f32[8,128]{1,0:T(8,128)S(1)}, f32[8,128]{1,0:T(8,128)S(1)}, bf16[4,512,128]{2,1,0:T(8,128)(2,1)}, ...), condition=%wide.region_5.6_spmd, body=%wide.region_2.5_spmd.sunk | while | flops 136841216 | bytes 4640849 | solution.py:52
  33.3 11.7 %while.69 = (s32[]{:T(128)}, f32[8,128]{1,0:T(8,128)S(1)}, bf16[4,512,128]{2,1,0:T(8,128)(2,1)}, bf16[128,8,128]{2,0,1:T(8,128)(2,1)S(1)}, f32[8,128]{1,0:T(8,12...) while((s32[]{:T(128)}, f32[8,128]{1,0:T(8,128)S(1)}, ...), condition=%wide.region_9.10_spmd, body=%wide.region_7.9_spmd.sunk | while | flops 271056896 | bytes 6054025 | solution.py:70
  37.7 1.5 fusion.190
  40.6 1.5 fusion.190
  43.6 1.5 fusion.190
  47.8 11.8 %while.72 = (s32[]{:T(128)}, f32[8,128]{1,0:T(8,128)S(1)}, bf16[4,512,128]{2,1,0:T(8,128)(2,1)}, bf16[128,8,128]{2,0,1:T(8,128)(2,1)S(1)}, f32[8,128]{1,0:T(8,12...) while((s32[]{:T(128)}, f32[8,128]{1,0:T(8,128)S(1)}, ...), condition=%wide.region_21.22_spmd, body=%wide.region_19.21_spmd.sunk | while | flops 271056896 | bytes 6054025 | solution.py:70
  52.1 1.5 fusion.212
  58.0 1.5 fusion.212
  60.9 1.5 broadcast.188.clone2
  62.4 32.5 %while.70 = (s32[]{:T(128)}, f32[128,8,128]{0,2,1:T(8,128)}, f32[4,512,256]{2,1,0:T(8,128)}, bf16[4,512,128]{2,1,0:T(8,128)(2,1)}, bf16[128,8,128]{0,2,1:T(8,128...) while((s32[]{:T(128)}, f32[128,8,128]{0,2,1:T(8,128)}, ...), condition=%wide.region_11.12_spmd, body=%wide.region_10.11_spmd.sunk | while | flops 675086336 | bytes 15609989 | solution.py:95
  62.4 1.5 fusion.201
  67.2 2.2 fusion.203
  70.5 1.5 fusion.201
  75.3 2.2 fusion.203
  78.7 1.5 fusion.201
  83.5 2.2 fusion.203
  86.8 1.5 fusion.201
  91.6 2.2 fusion.203
  94.9 1.5 broadcast.188.clone2.1
  96.5 28.6 %while.73 = (s32[]{:T(128)}, f32[128,8,128]{0,2,1:T(8,128)S(1)}, f32[4,512,256]{2,1,0:T(8,128)}, bf16[4,512,128]{2,1,0:T(8,128)(2,1)}, bf16[128,8,128]{0,2,1:T(8...) while((s32[]{:T(128)}, f32[128,8,128]{0,2,1:T(8,128)S(1)}, ...), condition=%wide.region_23.24_spmd, body=%wide.region_22.23_spmd.sunk | while | flops 675086336 | bytes 15609989 | solution.py:95
  96.5 1.5 fusion.223
  103.6 1.5 fusion.223
  110.8 1.5 fusion.223
  117.9 1.5 fusion.223
  125.0 4.7 %pad_maximum_fusion = f32[2048,512]{1,0:T(8,128)} fusion(f32[2048,256]{1,0:T(8,128)} %bitcast.354, f32[2048,256]{1,0:T(8,128)} %bitcast.355), kind=kLoop, calls=%fused_computation.92 | loop fusion | flops 1048576 | bytes 8388608 | tf_op jit(solution)/shard_map/concatenate | solution.py:180
  129.8 130.8 %reduce-scatter.8.cloned.1.call-done = f32[64,512]{1,0:T(8,128)} async-done(((f32[2048,512]{1,0:T(8,128)}), f32[64,512]{1,0:T(8,128)}) %reduce-scatter.8.cloned.1.call-update) | async-done | bytes 131088 | tf_op jit(solution)/shard_map/reduce_scatter | solution.py:182
  265.5 1.9 fusion.101
  278.1 23.8 %reduce-scatter.12.cloned.1.call-done = bf16[640,64]{1,0:T(8,128)(2,1)} async-done(((bf16[5120,64]{1,0:T(8,128)(2,1)}), bf16[640,64]{1,0:T(8,128)(2,1)}) %reduce-scatter.12.cloned.1.call-update) | async-done | bytes 81936
  302.9 42.9 %reduce-scatter.10.cloned.1.call-done = bf16[640,64]{1,0:T(8,128)(2,1)} async-done(((bf16[5120,64]{1,0:T(8,128)(2,1)}), bf16[640,64]{1,0:T(8,128)(2,1)}) %reduce-scatter.10.cloned.1.call-update) | async-done | bytes 81936
  347.1 19.3 %all-reduce = (f32[64]{0:T(128)S(1)}, f32[64]{0:T(128)S(1)}, f32[64]{0:T(128)S(1)}, f32[64]{0:T(128)S(1)}) all-reduce(f32[64]{0:T(128)S(1)} %get-tuple-element.417, f32[64]{0:T(128)S(1)} %get-tuple-element.416, f32[64]{0:T(128)S(1)} %get-tuple-element.415, f32[64]{0:T(128)S(1)} %get-tuple-element.414), channel_id=1, replica_groups=mesh['resp'=32,'head'=8] {'head'}, use_global_device_ids=true, to_apply=%region_34.35 | all-reduce | flops 256 | bytes 2048 | tf_op jit(solution)/shard_map/psum | solution.py:127
  (224 shorter events, 101.3 us)
Async XLA Ops:
  7.2 254.5 %copy-start = (bf16[5120,128]{1,0:T(8,128)(2,1)S(1)}, bf16[5120,128]{1,0:T(8,128)(2,1)}, u32[]{:S(2)}) copy-start(bf16[5120,128]{1,0:T(8,128)(2,1)} %param.44) | copy-start | bytes 3932164
  7.2 5.2 %copy-start.14 = (bf16[128,1024]{1,0:T(8,128)(2,1)S(1)}, bf16[128,1024]{1,0:T(8,128)(2,1)}, u32[]{:S(2)}) copy-start(bf16[128,1024]{1,0:T(8,128)(2,1)} %param.48) | copy-start | bytes 786436
  7.2 7.1 %copy-start.15 = (bf16[128,1024]{1,0:T(8,128)(2,1)S(1)}, bf16[128,1024]{1,0:T(8,128)(2,1)}, u32[]{:S(2)}) copy-start(bf16[128,1024]{1,0:T(8,128)(2,1)} %param.51) | copy-start | bytes 786436
  7.2 253.5 %reduce-scatter.8.cloned.1.call-start = ((), (), s32[]{:S(2)}) async-start(), calls=%async_computation.3 | async-start | bytes 4325376 | tf_op jit(solution)/shard_map/reduce_scatter | solution.py:182
  7.3 8.0 %copy-start.19 = (bf16[128,128]{1,0:T(8,128)(2,1)S(1)}, bf16[128,128]{1,0:T(8,128)(2,1)}, u32[]{:S(2)}) copy-start(bf16[128,128]{1,0:T(8,128)(2,1)} %param.49) | copy-start | bytes 98308
  16.6 43.0 %copy-start.1 = (f32[8,128,128]{1,2,0:T(8,128)}, f32[8,128,128]{1,2,0:T(8,128)S(1)}, u32[]{:S(2)}) copy-start(f32[8,128,128]{1,2,0:T(8,128)S(1)} %get-tuple-element.527) | copy-start | bytes 1572868
  16.7 7.2 %copy-start.18 = (bf16[128,128]{1,0:T(8,128)(2,1)S(1)}, bf16[128,128]{1,0:T(8,128)(2,1)}, u32[]{:S(2)}) copy-start(bf16[128,128]{1,0:T(8,128)(2,1)} %param.39) | copy-start | bytes 98308
  25.0 20.0 %copy-start.3 = (f32[8,128,128]{1,2,0:T(8,128)}, f32[8,128,128]{1,2,0:T(8,128)S(1)}, u32[]{:S(2)}) copy-start(f32[8,128,128]{1,2,0:T(8,128)S(1)} %get-tuple-element.523) | copy-start | bytes 1572868
  25.2 7.2 %copy-start.22 = (bf16[128,128]{1,0:T(8,128)(2,1)S(1)}, bf16[128,128]{1,0:T(8,128)(2,1)}, u32[]{:S(2)}) copy-start(bf16[128,128]{1,0:T(8,128)(2,1)} %param.40) | copy-start | bytes 98308
  33.3 1.4 copy-start.17
  36.3 1.4 copy-start.17
  39.2 1.4 copy-start.17
  42.1 1.4 copy-start.17
  45.1 2.5 copy-start.23
  46.3 1.5 copy-start.5
  47.8 1.4 copy-start.16
  50.7 1.4 copy-start.16
  53.7 1.4 copy-start.16
  56.6 1.4 copy-start.16
  59.7 0.7 copy-start.7
  129.8 172.1 %reduce-scatter.12.cloned.1.call-start = ((), (), s32[]{:S(2)}) async-start(), calls=%async_computation.5 | async-start | bytes 1474560
  260.7 1.7 copy-start.9
  262.9 1.7 copy-start.4
  264.4 81.4 %reduce-scatter.10.cloned.1.call-start = ((), (), s32[]{:S(2)}) async-start(), calls=%async_computation.4 | async-start | bytes 1474560
  264.6 2.8 copy-start.10
  268.7 1.5 copy-start.6
  268.7 2.7 copy-start.20
  268.7 2.7 copy-start.21
  268.8 5.4 %copy-start.2 = (f32[8,128,128]{1,2,0:T(8,128)S(1)}, f32[8,128,128]{1,2,0:T(8,128)}, u32[]{:S(2)}) copy-start(f32[8,128,128]{1,2,0:T(8,128)} %copy-done.1) | copy-start | bytes 1572868
  270.2 2.8 copy-start.8
  274.5 72.4 %copy-start.12 = (bf16[64,640]{1,0:T(8,128)(2,1)S(1)}, bf16[64,640]{1,0:T(8,128)(2,1)}, u32[]{:S(2)}) copy-start(bf16[64,640]{1,0:T(8,128)(2,1)} %param.42) | copy-start | bytes 245764
  274.5 72.5 %copy-start.11 = (bf16[64,640]{1,0:T(8,128)(2,1)S(1)}, bf16[64,640]{1,0:T(8,128)(2,1)}, u32[]{:S(2)}) copy-start(bf16[64,640]{1,0:T(8,128)(2,1)} %param.32) | copy-start | bytes 245764
  (1 other events, 0.6 us)
Sparse Core Ops, SparseCore 0:
  129.9 130.7 reduce-scatter.7
  264.5 37.3 reduce-scatter.11
  304.6 41.1 reduce-scatter.9
where the time goes:
time: 376 us; the launch traced here: 374 us
  waiting for transfers between devices  198 us (53%)
  matrix products  98.1 us (26%)
  local copies, waits for them, and re-layouts  29.6 us (8%)
  blocking collectives  19.3 us (5%)
  between operations  14.2 us (4%)
  other arithmetic  13.6 us (4%)
    reduce_scatter x1, waiting for transfers between devices, body(): lax.psum_scatter(joined, 'resp', scatter_dimension=0, tiled=True)  131 us
    unnamed x5, waiting for transfers between devices  66.7 us
    dot_general x24, matrix products, scores(): jnp.einsum('tgd,jd->gtj', query_rows, key_block, preferred_element_type=j...  34.2 us
    psum x1, blocking collectives, hidden_grad(): row_sums = lax.psum(jnp.sum(scaled * hidden, axis=1), 'head')  19.3 us
    dot_general x8, matrix products, backward(): jnp.einsum('gtj,jd->tgd', slopes, items[0], preferred_element_type=jnp.fl...  14 us
    dot_general x8, matrix products, accumulate(): jnp.einsum('tgd,jd->gtj', grad_rows, items[1], preferred_element_type=jnp...  12 us
    dot_general x8, matrix products, backward(): jnp.einsum('gtj,tgd->jd', slopes, query_rows, preferred_element_type=jnp....  11.4 us
    unnamed x54, local copies, waits for them, and re-layouts  11.3 us
  transfers between devices with their start and end apart: 3, of which 3 were waited for; matrix products, arithmetic and copies ran while one was open for 4% of the time, Pallas kernels for 0%

commit v1 on v0

v1 whole, which is shorter than its diff:
```python
import jax
import jax.numpy as jnp
from jax import lax
from jax.experimental import pallas as pl
from jax.experimental.pallas import tpu as pltpu

HEAD = 128
C = 64
NT = (((1,), (1,)), ((), ()))


def attend_kernel(q_ref, g_ref, k_ref, v_ref, sk_ref, sv_ref, dq_ref, span_ref, kv_ref,
                  keys, values, keys_t, scores, dots, slopes, weights, queries, grads):
    step = pl.program_id(0)
    steps = pl.num_programs(0)
    tokens = q_ref.shape[0]
    pair = 2 * tokens
    prompt = k_ref.shape[0]
    rows = prompt + tokens
    scale = HEAD ** -0.5
    factor = scale * 1.4426950408889634
    chunk = 128
    count = rows // chunk

    @pl.when(step == 0)
    def _():
        keys[:prompt, :] = k_ref[...]
        keys[prompt:, :] = sk_ref[...]
        values[:prompt, :] = v_ref[...]
        values[prompt:, :] = sv_ref[...]
        for j in range(count):
            keys_t[:, j * chunk:(j + 1) * chunk] = keys[j * chunk:(j + 1) * chunk, :].T

    query = jnp.concatenate([q_ref[:, :HEAD], q_ref[:, HEAD:]], axis=0)
    grad = jnp.concatenate([g_ref[:, :HEAD], g_ref[:, HEAD:]], axis=0)
    place = pl.ds(pl.multiple_of(step * pair, pair), pair)
    queries[place, :] = query
    grads[place, :] = grad

    highest = jnp.full((8, pair), -1e30, jnp.float32)
    for j in range(count):
        part = slice(j * chunk, (j + 1) * chunk)
        block = lax.dot_general(keys[part, :], query, NT, preferred_element_type=jnp.float32)
        if j == count - 1:
            u = lax.broadcasted_iota(jnp.int32, block.shape, 0)
            t = lax.rem(lax.broadcasted_iota(jnp.int32, block.shape, 1), tokens)
            block = jnp.where((lax.div(u, C) == lax.div(t, C)) & (u <= t), block, -1e30)
        scores[part, :] = block
        highest = jnp.maximum(highest, jnp.max(block.reshape(chunk // 8, 8, pair), axis=0))
    highest = jnp.max(highest, axis=0, keepdims=True)

    total = jnp.zeros((8, pair), jnp.float32)
    delta = jnp.zeros((8, pair), jnp.float32)
    for j in range(count):
        part = slice(j * chunk, (j + 1) * chunk)
        block = jnp.exp2((scores[part, :] - highest) * factor)
        scores[part, :] = block
        dot = lax.dot_general(values[part, :], grad, NT, preferred_element_type=jnp.float32)
        dots[part, :] = dot
        total = total + jnp.sum(block.reshape(chunk // 8, 8, pair), axis=0)
        delta = delta + jnp.sum((block * dot).reshape(chunk // 8, 8, pair), axis=0)
    inverse = 1.0 / jnp.sum(total, axis=0, keepdims=True)
    delta = jnp.sum(delta, axis=0, keepdims=True) * inverse

    query_grad = jnp.zeros((HEAD, pair), jnp.float32)
    for j in range(count):
        part = slice(j * chunk, (j + 1) * chunk)
        weight = scores[part, :] * inverse
        slope = (weight * (dots[part, :] - delta)).astype(jnp.bfloat16)
        weights[part, place] = weight.astype(jnp.bfloat16)
        slopes[part, place] = slope
    query_grad = jnp.dot(keys_t[...], slopes[:, place], preferred_element_type=jnp.float32)
    query_grad = query_grad * scale
    dq_ref[:, :HEAD] = query_grad[:, :tokens].T.astype(jnp.bfloat16)
    dq_ref[:, HEAD:] = query_grad[:, tokens:].T.astype(jnp.bfloat16)

    @pl.when(step == steps - 1)
    def _():
        for j in range(count):
            part = slice(j * chunk, (j + 1) * chunk)
            key_part = jnp.dot(slopes[part, :], queries[...], preferred_element_type=jnp.float32)
            value_part = jnp.dot(weights[part, :], grads[...], preferred_element_type=jnp.float32)
            both = jnp.concatenate([key_part * scale, value_part], axis=1).astype(jnp.bfloat16)
            if j < count - 1:
                kv_ref[part, :] = both
            else:
                span_ref[...] = both


def attend(q, k, v, sk, sv, g):
    tokens = q.shape[0]
    heads = q.shape[1] // HEAD
    prompt = k.shape[0]
    rows = prompt + tokens
    pair = 2 * tokens
    whole = lambda shape: pl.BlockSpec(shape, lambda i: (0, 0))
    paired = pl.BlockSpec((tokens, 2 * HEAD), lambda i: (0, i))
    return pl.pallas_call(
        attend_kernel,
        grid=(heads // 2,),
        in_specs=[paired, paired, whole((prompt, HEAD)), whole((prompt, HEAD)),
                  whole((tokens, HEAD)), whole((tokens, HEAD))],
        out_specs=[paired, whole((tokens, 2 * HEAD)), whole((prompt, 2 * HEAD))],
        out_shape=[
            jax.ShapeDtypeStruct(q.shape, jnp.bfloat16),
            jax.ShapeDtypeStruct((tokens, 2 * HEAD), jnp.bfloat16),
            jax.ShapeDtypeStruct((prompt, 2 * HEAD), jnp.bfloat16),
        ],
        scratch_shapes=[
            pltpu.VMEM((rows, HEAD), jnp.bfloat16),
            pltpu.VMEM((rows, HEAD), jnp.bfloat16),
            pltpu.VMEM((HEAD, rows), jnp.bfloat16),
            pltpu.VMEM((rows, pair), jnp.float32),
            pltpu.VMEM((rows, pair), jnp.float32),
            pltpu.VMEM((rows, heads * tokens), jnp.bfloat16),
            pltpu.VMEM((rows, heads * tokens), jnp.bfloat16),
            pltpu.VMEM((heads * tokens, HEAD), jnp.bfloat16),
            pltpu.VMEM((heads * tokens, HEAD), jnp.bfloat16),
        ],
        compiler_params=pltpu.CompilerParams(vmem_limit_bytes=48 * 1024 * 1024),
        cost_estimate=pl.CostEstimate(flops=10 * rows * heads * tokens * HEAD, bytes_accessed=4 * 2**20, transcendentals=rows * heads * tokens),
    )(q, g, k, v, sk, sv)


from jax.sharding import PartitionSpec as P

D = 5120
epsilon = 1e-06
RESP = 32
CORE_SWAP = [(i, i ^ 1) for i in range(RESP)]
SAME_CORE = [[2 * i + c for i in range(RESP // 2)] for c in range(2)]


def reduce_resp(upper_kv, lower_kv):
    core = lax.rem(lax.axis_index("resp"), 2)
    parts = []
    for kv in (upper_kv, lower_kv):
        blocks = kv.reshape(RESP // 2, 2, -1, kv.shape[1])
        mine = lax.dynamic_index_in_dim(blocks, core, 1, keepdims=False)
        other = lax.dynamic_index_in_dim(blocks, 1 - core, 1, keepdims=False)
        got = lax.ppermute(other, "resp", CORE_SWAP)
        total = mine.astype(jnp.float32) + got.astype(jnp.float32)
        parts.append(total.astype(jnp.bfloat16))
    sent = jnp.stack(parts, axis=1)
    blocks = lax.all_to_all(sent, "resp", 0, 0, axis_index_groups=SAME_CORE)
    return jnp.sum(blocks.astype(jnp.float32), axis=0)


def head_part(rows, key_weight, value_weight, hidden, gain):
    rounded = rows.astype(jnp.bfloat16)
    projected = lax.dot_general(
        rounded[:, :HEAD], key_weight, NT, preferred_element_type=jnp.float32
    ) + lax.dot_general(rounded[:, HEAD:], value_weight, NT, preferred_element_type=jnp.float32)
    hidden = hidden.astype(jnp.float32)
    inverse = lax.rsqrt(jnp.mean(hidden * hidden, axis=1, keepdims=True) + epsilon)
    scaled = gain.astype(jnp.float32) * projected
    row_sums = jnp.sum(scaled * hidden, axis=1, keepdims=True)
    return inverse * scaled - hidden * (inverse**3 * row_sums / D)


def body(
    upper_input, upper_gain, upper_key_weight, upper_value_weight, upper_prompt_keys,
    upper_prompt_values, upper_queries, upper_span_keys, upper_span_values, upper_out_grad,
    lower_input, lower_gain, lower_key_weight, lower_value_weight, lower_prompt_keys,
    lower_prompt_values, lower_queries, lower_span_keys, lower_span_values, lower_out_grad,
):
    rows = upper_input.shape[0]
    width = upper_input.shape[1]
    packed = jnp.concatenate(
        [upper_input, lower_input, upper_gain[None], lower_gain[None]], axis=0
    )
    whole = lax.all_gather(packed, "head", axis=1, tiled=True)
    upper_query, upper_span, upper_kv = attend(
        upper_queries, upper_prompt_keys, upper_prompt_values, upper_span_keys,
        upper_span_values, upper_out_grad,
    )
    lower_query, lower_span, lower_kv = attend(
        lower_queries, lower_prompt_keys, lower_prompt_values, lower_span_keys,
        lower_span_values, lower_out_grad,
    )
    summed = reduce_resp(upper_kv, lower_kv)
    part = head_part(
        summed[0], upper_key_weight, upper_value_weight, whole[:rows], whole[2 * rows : 2 * rows + 1]
    ) + head_part(
        summed[1], lower_key_weight, lower_value_weight, whole[rows : 2 * rows], whole[2 * rows + 1 :]
    )
    blocks = part.astype(jnp.bfloat16).reshape(rows, -1, width).transpose(1, 0, 2)
    blocks = lax.all_to_all(blocks, "head", 0, 0)
    prompt_grads = jnp.sum(blocks.astype(jnp.float32), axis=0).astype(jnp.bfloat16)
    return (upper_query, lower_query, upper_span, lower_span, prompt_grads)


def solution(mesh):
    layer = (
        P("resp", "head"), P("head"), P(None, "head"), P(None, "head"), P(None, "head"),
        P(None, "head"), P("resp", "head"), P("resp", "head"), P("resp", "head"), P("resp", "head"),
    )
    return jax.shard_map(
        body,
        mesh=mesh,
        in_specs=layer + layer,
        out_specs=(P("resp", "head"),) * 5,
        check_vma=False,
    )
```

time: 376 us -> 120 us (0.32)
  waiting for transfers between devices: 198 us -> 28.8 us
  matrix products: 98.1 us -> 4.06 us
  Pallas kernels: 0 us -> 25.2 us
  local copies, waits for them, and re-layouts: 29.6 us -> 14.2 us
  starting transfers between devices: 0.3 us -> 11.8 us
  blocking collectives: 19.3 us -> 13 us
  other arithmetic: 13.6 us -> 7.45 us
    reduce_scatter x1 -> x0, waiting for transfers between devices: 131 us -> none  [body(): lax.psum_scatter(joined, 'resp', scatter_dimension=0, tiled=True)]
    dot_general x78 -> x4, matrix products: 98.1 us -> 4.06 us  [the longest x2 2.56 us: head_part(): lax.dot_general(rounded[:, :HEAD], key_weight, NT, preferred_element_type...]
    unnamed x5 -> x1, waiting for transfers between devices: 66.7 us -> 0.02 us
    all_to_all x0 -> x1, waiting for transfers between devices: none -> 28.1 us  [reduce_resp(): blocks = lax.all_to_all(sent, 'resp', 0, 0, axis_index_groups=SAME_CORE)]
    pallas_call x0 -> x2, Pallas kernels: none -> 25.2 us  [attend(): pl.pallas_call(attend_kernel, grid=(heads // 2,), in_specs=[paired, paire...]
    psum x1 -> x0, blocking collectives: 19.3 us -> none  [hidden_grad(): row_sums = lax.psum(jnp.sum(scaled * hidden, axis=1), 'head')]
    all_to_all x0 -> x1, blocking collectives: none -> 13 us  [body(): blocks = lax.all_to_all(blocks, 'head', 0, 0)]
    all_to_all x0 -> x1, starting transfers between devices: none -> 11.2 us  [reduce_resp(): blocks = lax.all_to_all(sent, 'resp', 0, 0, axis_index_groups=SAME_CORE)]
  transfers between devices with their start and end apart: 3 -> 4, of which waited for: 3 -> 2; matrix products, arithmetic and copies ran while one was open for 4% -> 5% of each run, Pallas kernels for 0% -> 21%
where the time goes in v1:
time: 120 us; the launch traced here: 119 us
  waiting for transfers between devices  28.8 us (24%)
  Pallas kernels  25.2 us (21%)
  local copies, waits for them, and re-layouts  14.2 us (12%)
  between operations  14.2 us (12%)
  blocking collectives  13 us (11%)
  starting transfers between devices  11.8 us (10%)
  other arithmetic  7.45 us (6%)
  matrix products  4.06 us (3%)
    all_to_all x1, waiting for transfers between devices, reduce_resp(): blocks = lax.all_to_all(sent, 'resp', 0, 0, axis_index_groups=SAME_CORE)  28.1 us
    pallas_call x2, Pallas kernels, attend(): pl.pallas_call(attend_kernel, grid=(heads // 2,), in_specs=[paired, paire...  25.2 us
    all_to_all x1, blocking collectives, body(): blocks = lax.all_to_all(blocks, 'head', 0, 0)  13 us
    all_to_all x1, starting transfers between devices, reduce_resp(): blocks = lax.all_to_all(sent, 'resp', 0, 0, axis_index_groups=SAME_CORE)  11.2 us
    unnamed x32, local copies, waits for them, and re-layouts  11 us
    another operation x3, other arithmetic, reduce_resp(): sent = jnp.stack(parts, axis=1)  3.45 us
    dot_general x2, matrix products, head_part(): lax.dot_general(rounded[:, :HEAD], key_weight, NT, preferred_element_type...  2.56 us
  transfers between devices with their start and end apart: 4, of which 2 were waited for; matrix products, arithmetic and copies ran while one was open for 5% of the time, Pallas kernels for 21%

profile of v1, /device:TPU:2, one launch (start us, length us, event | category | flops | bytes accessed | tf_op | source)
XLA Modules:
  0.0 118.7 jit_solution(12524282383549012001)
XLA Ops:
  7.2 0.8 broadcast_in_dim.4
  8.0 0.7 broadcast_in_dim.5
  8.7 1.6 %pad_maximum_fusion.1 = bf16[130,640]{1,0:T(8,128)(2,1)} fusion(bf16[1,640]{1,0:T(2,128)(2,1)S(1)} %broadcast_in_dim.5, bf16[1,640]{1,0:T(2,128)(2,1)S(1)} %broadcast_in_dim.4, bf16[64,640]{1,0:T(8,128)(2,1)} %param.30, bf16[64,640]{1,0:T(8,128)(2,1)} %param.20), kind=kLoop, calls=%fused_computation.28 | loop fusion | flops 665600 | bytes 332800 | tf_op jit(solution)/shard_map/concatenate | solution.py:169
  10.4 1.0 copy-done.1
  11.4 1.0 copy-done.2
  12.4 0.9 copy-done.5
  13.4 0.9 copy-done.6
  14.3 0.8 copy-done.9
  15.1 0.8 copy-done.10
  15.9 12.6 %shard_map.227 = (bf16[128,1024]{1,0:T(8,128)(2,1)}, bf16[128,256]{1,0:T(8,128)(2,1)}, bf16[2048,256]{1,0:T(8,128)(2,1)S(1)}) custom-call(bf16[128,1024]{1,0:T(8,128)(2,1)S(1)} %copy-done.5, bf16[128,1024]{1,0:T(8,128)(2,1)S(1)} %copy-done.6, bf16[2048,128]{1,0:T(8,128)(2,1)S(1)} %copy-done.1, bf16[2048,128]{1,0:T(8,128)(2,1)S(1)} %copy-done.2, ...), custom_call_target="tpu_custom_call" | custom-call | flops 2852126720 | bytes 4194304 | tf_op jit(solution)/shard_map/pallas_call | solution.py:98
  28.5 0.8 dynamic-slice_bitcast_fusion.1
  29.3 1.0 copy-done.3
  30.4 1.0 copy-done.4
  31.4 0.9 copy-done.7
  32.4 0.9 copy-done.8
  33.3 12.6 %shard_map.228 = (bf16[128,1024]{1,0:T(8,128)(2,1)}, bf16[128,256]{1,0:T(8,128)(2,1)}, bf16[2048,256]{1,0:T(8,128)(2,1)S(1)}) custom-call(bf16[128,1024]{1,0:T(8,128)(2,1)S(1)} %copy-done.7, bf16[128,1024]{1,0:T(8,128)(2,1)S(1)} %copy-done.8, bf16[2048,128]{1,0:T(8,128)(2,1)S(1)} %copy-done.3, bf16[2048,128]{1,0:T(8,128)(2,1)S(1)} %copy-done.4, ...), custom_call_target="tpu_custom_call" | custom-call | flops 2852126720 | bytes 4194304 | tf_op jit(solution)/shard_map/pallas_call | solution.py:98
  45.9 0.8 dynamic-slice_bitcast_fusion
  47.3 1.2 %fusion.12 = bf16[16,1,64,256]{3,2,1,0:T(8,128)(2,1)S(1)} fusion(bf16[16,64,256]{2,1,0:T(8,128)(2,1)} %collective-permute-done, bf16[16,2,64,256]{3,2,1,0:T(8,128)(2,1)S(1)} %bitcast.38, s32[]{:T(128)S(6)} %select_n.9), kind=kLoop, calls=%fused_computation.24 | loop fusion | flops 1048576 | bytes 1572868 | tf_op jit(solution)/shard_map/stack | solution.py:144
  48.5 0.7 collective-permute-done.1
  49.1 1.2 %fusion.13 = bf16[16,1,64,256]{3,2,1,0:T(8,128)(2,1)S(1)} fusion(bf16[16,64,256]{2,1,0:T(8,128)(2,1)} %collective-permute-done.1, bf16[16,2,64,256]{3,2,1,0:T(8,128)(2,1)S(1)} %bitcast.40, s32[]{:T(128)S(6)} %select_n.9), kind=kLoop, calls=%fused_computation.25 | loop fusion | flops 1048576 | bytes 1572868 | tf_op jit(solution)/shard_map/stack | solution.py:144
  50.3 1.1 pad_maximum_fusion
  51.4 11.2 %all-to-all-start = ((bf16[16,2,64,256]{3,2,1,0:T(8,128)(2,1)}), bf16[16,2,64,256]{3,2,1,0:T(8,128)(2,1)S(1)}, u32[]{:S(2)}, u32[]{:S(2)}) async-start(bf16[16,2,64,256]{3,2,1,0:T(8,128)(2,1)} %pad_maximum_fusion), calls=%async_computation | async-start | bytes 2097152 | tf_op jit(solution)/shard_map/all_to_all | solution.py:145
  62.7 1.0 slice_convert_fusion.1
  63.7 28.1 %all-to-all-done = bf16[16,2,64,256]{3,2,1,0:T(8,128)(2,1)S(1)} async-done(((bf16[16,2,64,256]{3,2,1,0:T(8,128)(2,1)}), bf16[16,2,64,256]{3,2,1,0:T(8,128)(2,1)S(1)}, u32[]{:S(2)}, u32[]{:S(2)}) %all-to-all-start) | async-done | bytes 1048608 | tf_op jit(solution)/shard_map/all_to_all | solution.py:145
  92.0 2.0 %fusion.18 = f32[64,5120]{1,0:T(8,128)S(1)} fusion(bf16[5120,128]{1,0:T(8,128)(2,1)} %param.22, bf16[64,256]{1,0:T(8,128)(2,1)S(1)} %get-tuple-element.23), kind=kOutput, calls=%fused_computation.37 | convolution fusion | flops 83886080 | bytes 2637824 | tf_op jit(solution)/shard_map/dot_general | solution.py:151
  94.0 0.6 fusion.15
  94.6 0.7 copy-done.14
  95.3 0.6 fusion
  95.9 0.7 copy-done.13
  96.6 0.9 fusion.2
  98.2 13.0 %all_to_all.10 = bf16[8,64,640]{2,1,0:T(8,128)(2,1)S(1)} all-to-all(bf16[8,64,640]{2,1,0:T(8,128)(2,1)S(1)} %bitcast.41), channel_id=1, replica_groups=mesh['resp'=32,'head'=8] {'head'}, dimensions={0} | all-to-all | bytes 1310720 | tf_op jit(solution)/shard_map/all_to_all | solution.py:188
  111.1 0.7 reduce_sum.62
  (31 shorter events, 1.4 us)
Async XLA Ops:
  7.2 88.7 %copy-start = (bf16[5120,128]{1,0:T(8,128)(2,1)S(1)}, bf16[5120,128]{1,0:T(8,128)(2,1)}, u32[]{:S(2)}) copy-start(bf16[5120,128]{1,0:T(8,128)(2,1)} %param.23) | copy-start | bytes 3932164
  7.2 55.5 %all-gather.2.cloned.1.call-start = ((), (), s32[]{:S(2)}) async-start(), calls=%async_computation.2 | async-start | bytes 1566720 | tf_op jit(solution)/shard_map/all_gather | solution.py:172
  10.3 1.0 copy-start.1
  11.4 1.0 copy-start.2
  12.4 0.9 copy-start.5
  13.4 0.9 copy-start.6
  14.3 0.8 copy-start.9
  15.1 0.8 copy-start.10
  15.8 13.5 %copy-start.11 = (bf16[128,128]{1,0:T(8,128)(2,1)S(1)}, bf16[128,128]{1,0:T(8,128)(2,1)}, u32[]{:S(2)}) copy-start(bf16[128,128]{1,0:T(8,128)(2,1)} %sk_ref.3) | copy-start | bytes 98308
  15.9 13.5 %copy-start.12 = (bf16[128,128]{1,0:T(8,128)(2,1)S(1)}, bf16[128,128]{1,0:T(8,128)(2,1)}, u32[]{:S(2)}) copy-start(bf16[128,128]{1,0:T(8,128)(2,1)} %sv_ref.3) | copy-start | bytes 98308
  29.3 18.0 %collective-permute-start = (bf16[16,64,256]{2,1,0:T(8,128)(2,1)}, bf16[16,64,256]{2,1,0:T(8,128)(2,1)}, u32[]{:S(2)}, u32[]{:S(2)}) collective-permute-start(bf16[16,64,256]{2,1,0:T(8,128)(2,1)} %dynamic-slice_bitcast_fusion.1), channel_id=1, source_target_pairs={{0,8},{8,0},{16,24},{24,16},{32,40},{40,32},{48,56},{56,48},{64,72... | collective-permute-start | bytes 1572872 | tf_op jit(solution)/shard_map/ppermute | solution.py:141
  29.3 1.0 copy-start.3
  30.4 1.0 copy-start.4
  31.4 0.9 copy-start.7
  32.3 0.9 copy-start.8
  46.7 2.4 %collective-permute-start.1 = (bf16[16,64,256]{2,1,0:T(8,128)(2,1)}, bf16[16,64,256]{2,1,0:T(8,128)(2,1)}, u32[]{:S(2)}, u32[]{:S(2)}) collective-permute-start(bf16[16,64,256]{2,1,0:T(8,128)(2,1)} %dynamic-slice_bitcast_fusion), channel_id=1, source_target_pairs={{0,8},{8,0},{16,24},{24,16},{32,40},{40,32},{48,56},{56,48},{64,72... | collective-permute-start | bytes 1572872 | tf_op jit(solution)/shard_map/ppermute | solution.py:141
  51.4 40.4 %all-to-all-start = ((bf16[16,2,64,256]{3,2,1,0:T(8,128)(2,1)}), bf16[16,2,64,256]{3,2,1,0:T(8,128)(2,1)S(1)}, u32[]{:S(2)}, u32[]{:S(2)}) async-start(bf16[16,2,64,256]{3,2,1,0:T(8,128)(2,1)} %pad_maximum_fusion), calls=%async_computation | async-start | bytes 2097152 | tf_op jit(solution)/shard_map/all_to_all | solution.py:145
  92.0 2.0 %copy-start.15 = (bf16[5120,128]{1,0:T(8,128)(2,1)S(1)}, bf16[5120,128]{1,0:T(8,128)(2,1)}, u32[]{:S(2)}) copy-start(bf16[5120,128]{1,0:T(8,128)(2,1)} %param.32) | copy-start | bytes 3932164
  94.0 1.3 %copy-start.14 = (bf16[5120,128]{1,0:T(8,128)(2,1)S(1)}, bf16[5120,128]{1,0:T(8,128)(2,1)}, u32[]{:S(2)}) copy-start(bf16[5120,128]{1,0:T(8,128)(2,1)} %param.33) | copy-start | bytes 3932164
  95.3 1.3 %copy-start.13 = (bf16[130,5120]{1,0:T(8,128)(2,1)S(1)}, bf16[130,5120]{1,0:T(8,128)(2,1)}, u32[]{:S(2)}) copy-start(bf16[130,5120]{1,0:T(8,128)(2,1)} %all-gather.2.cloned.1.call-done) | copy-start | bytes 3993604
Sparse Core Ops, SparseCore 0:
  10.5 42.9 all-gather.1

commit v2 on v1

v2 whole, which is shorter than its diff:
```python
import functools
import jax
import jax.numpy as jnp
from jax import lax
from jax.experimental import pallas as pl
from jax.experimental.pallas import tpu as pltpu
from jax.sharding import PartitionSpec as P

HEAD = 128
C = 64
NT = (((1,), (1,)), ((), ()))
TN = (((0,), (0,)), ((), ()))


def attend_kernel(core_ref, q_ref, g_ref, k_ref, v_ref, sk_ref, sv_ref, dq_ref, span_ref,
                  mine_ref, other_ref, scores, dots, key_sums, value_sums):
    tokens = q_ref.shape[0]
    prompt = k_ref.shape[0]
    group = 2
    pair = group * tokens
    pairs = q_ref.shape[1] // (group * HEAD)
    scale = HEAD ** -0.5
    factor = scale * 1.4426950408889634
    chunk = 2 * C
    count = prompt // chunk + 1
    parts = [slice(j * chunk, (j + 1) * chunk) for j in range(count)]
    even = core_ref[0] == 0

    def rows_of(ref, span, j):
        return ref[parts[j], :] if j < count - 1 else span[...]

    def stacked(ref, p):
        heads = [ref[:, h * HEAD:(h + 1) * HEAD] for h in range(group * p, group * p + group)]
        return jnp.concatenate(heads, axis=0)

    def first_pass(p, state):
        query = stacked(q_ref, p)
        grad = stacked(g_ref, p)
        tops = []
        totals = []
        deltas = []
        for j in range(count):
            block = lax.dot_general(
                rows_of(k_ref, sk_ref, j), query, NT, preferred_element_type=jnp.float32
            )
            if j == count - 1:
                u = lax.broadcasted_iota(jnp.int32, block.shape, 0)
                t = lax.rem(lax.broadcasted_iota(jnp.int32, block.shape, 1), tokens)
                block = jnp.where((lax.div(u, C) == lax.div(t, C)) & (u <= t), block, -1e30)
            top = jnp.max(block, axis=0, keepdims=True)
            block = jnp.exp2((block - top) * factor)
            scores[p, parts[j], :] = block
            dot = lax.dot_general(
                rows_of(v_ref, sv_ref, j), grad, NT, preferred_element_type=jnp.float32
            )
            dots[p, parts[j], :] = dot
            tops.append(top)
            totals.append(jnp.sum(block, axis=0, keepdims=True))
            deltas.append(jnp.sum(block * dot, axis=0, keepdims=True))
            yield
        tops = jnp.concatenate(tops, axis=0)
        weigh = jnp.exp2((tops - jnp.max(tops, axis=0, keepdims=True)) * factor)
        total = jnp.sum(weigh * jnp.concatenate(totals, axis=0), axis=0, keepdims=True)
        weigh = weigh / total
        delta = jnp.sum(weigh * jnp.concatenate(deltas, axis=0), axis=0, keepdims=True)
        state[p] = (query, grad, weigh, delta)

    def second_pass(p, state):
        query, grad, weigh, delta = state.pop(p)
        query_grad = jnp.zeros((pair, HEAD), jnp.float32)
        for j in range(count):
            weight = scores[p, parts[j], :] * weigh[j:j + 1, :]
            slope = (weight * (dots[p, parts[j], :] - delta)).astype(jnp.bfloat16)
            weight = weight.astype(jnp.bfloat16)
            query_grad = query_grad + lax.dot_general(
                slope, rows_of(k_ref, sk_ref, j), TN, preferred_element_type=jnp.float32
            )
            key_sum = jnp.dot(slope, query, preferred_element_type=jnp.float32)
            value_sum = jnp.dot(weight, grad, preferred_element_type=jnp.float32)
            if p > 0:
                key_sum = key_sum + key_sums[parts[j], :]
                value_sum = value_sum + value_sums[parts[j], :]
            if p < pairs - 1:
                key_sums[parts[j], :] = key_sum
                value_sums[parts[j], :] = value_sum
            else:
                both = jnp.concatenate([key_sum * scale, value_sum], axis=1)
                if j == count - 1:
                    span_ref[...] = both.astype(jnp.bfloat16)
                else:
                    half = slice(j * C, (j + 1) * C)
                    mine_ref[half, :] = jnp.where(even, both[:C], both[C:]).astype(jnp.bfloat16)
                    other_ref[half, :] = jnp.where(even, both[C:], both[:C]).astype(jnp.bfloat16)
            yield
        query_grad = query_grad * scale
        for h in range(group):
            place = (group * p + h) * HEAD
            dq_ref[:, place:place + HEAD] = query_grad[h * tokens:(h + 1) * tokens].astype(jnp.bfloat16)

    state = {}
    for p in range(pairs + 1):
        passes = []
        if p > 0:
            passes.append(second_pass(p - 1, state))
        if p < pairs:
            passes.append(first_pass(p, state))
        while passes:
            for one in list(passes):
                if next(one, passes) is passes:
                    passes.remove(one)


def attend(core, q, k, v, sk, sv, g):
    tokens = q.shape[0]
    heads = q.shape[1] // HEAD
    prompt = k.shape[0]
    rows = prompt + tokens

    def whole(*shape):
        return pl.BlockSpec(shape, lambda i, core: (0, 0))

    paired = whole(tokens, heads * HEAD)
    return pl.pallas_call(
        attend_kernel,
        grid_spec=pltpu.PrefetchScalarGridSpec(
            num_scalar_prefetch=1,
            grid=(1,),
            in_specs=[
                paired, paired, whole(prompt, HEAD), whole(prompt, HEAD),
                whole(tokens, HEAD), whole(tokens, HEAD),
            ],
            out_specs=[
                paired, whole(tokens, 2 * HEAD), whole(prompt // 2, 2 * HEAD),
                whole(prompt // 2, 2 * HEAD),
            ],
            scratch_shapes=[
                pltpu.VMEM((heads // 2, rows, 2 * tokens), jnp.float32),
                pltpu.VMEM((heads // 2, rows, 2 * tokens), jnp.float32),
                pltpu.VMEM((rows, HEAD), jnp.float32),
                pltpu.VMEM((rows, HEAD), jnp.float32),
            ],
        ),
        out_shape=[
            jax.ShapeDtypeStruct(q.shape, jnp.bfloat16),
            jax.ShapeDtypeStruct((tokens, 2 * HEAD), jnp.bfloat16),
            jax.ShapeDtypeStruct((prompt // 2, 2 * HEAD), jnp.bfloat16),
            jax.ShapeDtypeStruct((prompt // 2, 2 * HEAD), jnp.bfloat16),
        ],
        compiler_params=pltpu.CompilerParams(vmem_limit_bytes=62 * 1024 * 1024),
        cost_estimate=pl.CostEstimate(
            flops=10 * rows * heads * tokens * HEAD,
            bytes_accessed=4 * 1024 * 1024,
            transcendentals=rows * heads * tokens,
        ),
    )(core, q, g, k, v, sk, sv)


D = 5120
epsilon = 1e-06
RESP = 32
HEADS = 8
CORE_SWAP = [(i, i ^ 1) for i in range(RESP)]
FAR_SWAP = [(i, i ^ 16) for i in range(RESP)]
SAME_CORE = [[2 * i + c for i in range(RESP // 2)] for c in range(2)]
NEAR_SWAP = [(i, i ^ 4) for i in range(HEADS)]
UP = [(i, i // 4 * 4 + (i + 1) % 4) for i in range(HEADS)]
DOWN = [(i, i // 4 * 4 + (i + 3) % 4) for i in range(HEADS)]
EXTRA = 16
SMEM = pl.BlockSpec(memory_space=pltpu.SMEM)
BIG_VMEM = pltpu.CompilerParams(vmem_limit_bytes=62 * 1024 * 1024)


def cost(read, flops=0):
    return pl.CostEstimate(flops=flops, bytes_accessed=read, transcendentals=0)


def pack_kernel(upper_ref, lower_ref, upper_gain_ref, lower_gain_ref, out_ref):
    rows, width = upper_ref.shape
    place = lax.broadcasted_iota(jnp.int32, (EXTRA, width), 0)
    upper_gain = upper_gain_ref[...].astype(jnp.float32).reshape(1, width)
    lower_gain = lower_gain_ref[...].astype(jnp.float32).reshape(1, width)
    gains = jnp.where(place == 0, upper_gain, jnp.where(place == 1, lower_gain, 0.0))
    out_ref[:rows, :] = upper_ref[...]
    out_ref[rows : 2 * rows, :] = lower_ref[...]
    out_ref[2 * rows :, :] = gains.astype(jnp.bfloat16)


def pack(upper_input, lower_input, upper_gain, lower_gain):
    rows, width = upper_input.shape
    return pl.pallas_call(
        pack_kernel,
        out_shape=jax.ShapeDtypeStruct((2 * rows + EXTRA, width), jnp.bfloat16),
        compiler_params=BIG_VMEM,
        cost_estimate=cost(400000),
    )(upper_input, lower_input, upper_gain, lower_gain)


def split_kernel(far_ref, mine_ref, got_ref, own_ref, near_ref, kept_ref, sent_ref, both_ref):
    half = kept_ref.shape[1]
    low = far_ref[0] == 0
    for i in range(kept_ref.shape[0]):
        start = i * 2 * half
        one = mine_ref[start : start + half, :].astype(jnp.float32) + got_ref[
            start : start + half, :
        ].astype(jnp.float32)
        two = mine_ref[start + half : start + 2 * half, :].astype(jnp.float32) + got_ref[
            start + half : start + 2 * half, :
        ].astype(jnp.float32)
        kept_ref[i] = jnp.where(low, one, two).astype(jnp.bfloat16)
        sent_ref[i] = jnp.where(low, two, one).astype(jnp.bfloat16)
    both_ref[0] = own_ref[...]
    both_ref[1] = near_ref[...]


def split(far, mine, got, own, near):
    blocks = RESP // 2
    half = jax.ShapeDtypeStruct((blocks, mine.shape[0] // blocks // 2, mine.shape[1]), mine.dtype)
    vmem = pl.BlockSpec(memory_space=pltpu.VMEM)
    return pl.pallas_call(
        split_kernel,
        in_specs=[SMEM, vmem, vmem, vmem, vmem],
        out_shape=[half, half, jax.ShapeDtypeStruct((2,) + own.shape, own.dtype)],
        compiler_params=BIG_VMEM,
        cost_estimate=cost(3000000),
    )(far, mine, got, own, near)


def join_kernel(kept_ref, far_ref, mine_ref, got_ref, out_ref):
    half = kept_ref.shape[1]
    for i in range(kept_ref.shape[0]):
        part = slice(i * 2 * half, (i + 1) * 2 * half)
        upper = kept_ref[i].astype(jnp.float32) + far_ref[i].astype(jnp.float32)
        lower = mine_ref[part, :].astype(jnp.float32) + got_ref[part, :].astype(jnp.float32)
        out_ref[i, :half, :] = upper.astype(jnp.bfloat16)
        out_ref[i, half:, :] = lower.astype(jnp.bfloat16)


def join(kept, far, mine, got):
    blocks, half, width = kept.shape
    return pl.pallas_call(
        join_kernel,
        out_shape=jax.ShapeDtypeStruct((blocks, 3 * half, width), kept.dtype),
        compiler_params=BIG_VMEM,
        cost_estimate=cost(3000000),
    )(kept, far, mine, got)


def project_kernel(head_ref, blocks_ref, *refs):
    weight_refs = refs[:4]
    piece_refs = refs[4:8]
    out_ref, scaled = refs[8:]
    count, rows, width = out_ref.shape
    half = rows // 2
    sources = blocks_ref.shape[0]

    def total(first, last, part):
        summed = blocks_ref[first, part, :].astype(jnp.float32)
        for i in range(first + 1, last):
            summed = summed + blocks_ref[i, part, :].astype(jnp.float32)
        return summed.astype(jnp.bfloat16)

    upper = jnp.concatenate(
        [
            total(0, sources // 2, slice(0, half)),
            total(sources // 2, sources, slice(0, half)),
        ],
        axis=0,
    )
    lower = total(0, sources, slice(half, 3 * half))
    near = lax.div(head_ref[0], 4)
    across = lax.rem(head_ref[0], 4)
    pieces = []
    for piece_ref, shift in zip(piece_refs, (0, 3, 1, 2)):
        for j in range(2):
            side = near if j == 0 else 1 - near
            pieces.append((piece_ref, j, side * 4 + lax.rem(across + shift, 4)))
    stats = [[jnp.zeros((rows, 1), jnp.float32)] * 2 for layer in range(2)]
    for piece_ref, j, owner in pieces:
        columns = pl.ds(pl.multiple_of(owner * width, 128), width)
        gains = piece_ref[j, 2 * rows :, :].astype(jnp.float32)
        for layer, rounded in enumerate((upper, lower)):
            key_weight = weight_refs[2 * layer][columns, :]
            value_weight = weight_refs[2 * layer + 1][columns, :]
            projected = lax.dot_general(
                rounded[:, :HEAD], key_weight, NT, preferred_element_type=jnp.float32
            ) + lax.dot_general(
                rounded[:, HEAD:], value_weight, NT, preferred_element_type=jnp.float32
            )
            hidden = piece_ref[j, layer * rows : (layer + 1) * rows, :].astype(jnp.float32)
            one = projected * gains[layer : layer + 1]
            scaled[layer, owner] = one
            squares, sums = stats[layer]
            stats[layer] = [
                squares + jnp.sum(hidden * hidden, axis=1, keepdims=True),
                sums + jnp.sum(one * hidden, axis=1, keepdims=True),
            ]
    inverses = []
    shrinks = []
    for squares, sums in stats:
        inverse = lax.rsqrt(squares / D + epsilon)
        inverses.append(inverse)
        shrinks.append(inverse * inverse * inverse * sums / D)
    for piece_ref, j, owner in pieces:
        part = jnp.zeros((rows, width), jnp.float32)
        for layer in range(2):
            hidden = piece_ref[j, layer * rows : (layer + 1) * rows, :].astype(jnp.float32)
            part = part + inverses[layer] * scaled[layer, owner] - shrinks[layer] * hidden
        out_ref[owner] = part.astype(jnp.bfloat16)


def project(head, blocks, weights, pieces):
    rows = blocks.shape[1] // 3 * 2
    width = pieces[0].shape[2]
    vmem = pl.BlockSpec(memory_space=pltpu.VMEM)
    return pl.pallas_call(
        project_kernel,
        in_specs=[SMEM] + [vmem] * 9,
        out_shape=jax.ShapeDtypeStruct((HEADS, rows, width), jnp.bfloat16),
        scratch_shapes=[pltpu.VMEM((2, HEADS, rows, width), jnp.float32)],
        compiler_params=BIG_VMEM,
        cost_estimate=cost(8000000, 8 * rows * D * HEAD),
    )(head, blocks, *weights, *pieces)


def body(
    upper_input, upper_gain, upper_key_weight, upper_value_weight, upper_prompt_keys,
    upper_prompt_values, upper_queries, upper_span_keys, upper_span_values, upper_out_grad,
    lower_input, lower_gain, lower_key_weight, lower_value_weight, lower_prompt_keys,
    lower_prompt_values, lower_queries, lower_span_keys, lower_span_values, lower_out_grad,
):
    place = lax.axis_index("resp").astype(jnp.int32)
    core = lax.rem(place, 2).reshape(1)
    far = lax.div(place, 16).reshape(1)
    head = lax.axis_index("head").astype(jnp.int32).reshape(1)
    own = pack(upper_input, lower_input, upper_gain, lower_gain)
    own, upper_queries = lax.optimization_barrier((own, upper_queries))
    near = lax.ppermute(own, "head", NEAR_SWAP)
    upper_query, upper_span, mine, other = attend(
        core, upper_queries, upper_prompt_keys, upper_prompt_values, upper_span_keys,
        upper_span_values, upper_out_grad,
    )
    other, near = lax.optimization_barrier((other, near))
    got = lax.ppermute(other, "resp", CORE_SWAP)
    kept, sent, pair = split(far, mine, got, own, near)
    sent, pair, lower_queries = lax.optimization_barrier((sent, pair, lower_queries))
    from_far = lax.ppermute(sent, "resp", FAR_SWAP)
    from_below = lax.ppermute(pair, "head", UP)
    from_above = lax.ppermute(pair, "head", DOWN)
    lower_query, lower_span, mine, other = attend(
        core, lower_queries, lower_prompt_keys, lower_prompt_values, lower_span_keys,
        lower_span_values, lower_out_grad,
    )
    other, from_far, from_below, from_above = lax.optimization_barrier(
        (other, from_far, from_below, from_above)
    )
    got = lax.ppermute(other, "resp", CORE_SWAP)
    partial = join(kept, from_far, mine, got)
    from_across = lax.ppermute(from_below, "head", UP)
    blocks = lax.all_to_all(partial, "resp", 0, 0, axis_index_groups=SAME_CORE)
    part = project(
        head,
        blocks,
        (upper_key_weight, upper_value_weight, lower_key_weight, lower_value_weight),
        (pair, from_below, from_above, from_across),
    )
    blocks = lax.all_to_all(part, "head", 0, 0)
    prompt_grads = jnp.sum(blocks.astype(jnp.float32), axis=0).astype(jnp.bfloat16)
    return (upper_query, lower_query, upper_span, lower_span, prompt_grads)


def solution(mesh):
    layer = (
        P("resp", "head"), P("head"), P(None, "head"), P(None, "head"), P(None, "head"),
        P(None, "head"), P("resp", "head"), P("resp", "head"), P("resp", "head"), P("resp", "head"),
    )
    return jax.shard_map(
        body,
        mesh=mesh,
        in_specs=layer + layer,
        out_specs=(P("resp", "head"),) * 5,
        check_vma=False,
    )
```

time: 120 us -> 93.7 us (0.78)
  between operations: 14.2 us -> 0.72 us
  local copies, waits for them, and re-layouts: 14.2 us -> 2.51 us
  Pallas kernels: 25.2 us -> 33.1 us
  other arithmetic: 7.45 us -> 0.73 us
  starting transfers between devices: 11.8 us -> 16.9 us
  matrix products: 4.06 us -> 0 us
  waiting for transfers between devices: 28.8 us -> 25.9 us
    all_to_all x1, waiting for transfers between devices: 28.1 us -> 12.8 us  [body(): blocks = lax.all_to_all(partial, 'resp', 0, 0, axis_index_groups=SAME_CORE)]
    ppermute x2 -> x7, waiting for transfers between devices: 0.68 us -> 13.1 us  [the longest x1 8.86 us: body(): from_across = lax.ppermute(from_below, 'head', UP)]
    unnamed x32 -> x16, local copies, waits for them, and re-layouts: 11 us -> 2.51 us
    pallas_call x2 -> x6, Pallas kernels: 25.2 us -> 33.1 us  [the longest x2 19.8 us: attend(): pl.pallas_call(attend_kernel, grid_spec=pltpu.PrefetchScalarGridSpec(num_...]
    ppermute x2 -> x7, starting transfers between devices: 0.51 us -> 8.26 us  [the longest x1 2.9 us: body(): from_far = lax.ppermute(sent, 'resp', FAR_SWAP)]
    dot_general x4 -> x0, matrix products: 4.06 us -> none  [the longest x2 2.56 us: head_part(): lax.dot_general(rounded[:, :HEAD], key_weight, NT, preferred_element_type...]
    another operation x3 -> x0, other arithmetic: 3.45 us -> none  [reduce_resp(): sent = jnp.stack(parts, axis=1)]
    all_to_all x1, starting transfers between devices: 11.2 us -> 8.63 us  [body(): blocks = lax.all_to_all(partial, 'resp', 0, 0, axis_index_groups=SAME_CORE)]
  transfers between devices with their start and end apart: 4 -> 8, of which waited for: 2 -> 4; matrix products, arithmetic and copies ran while one was open for 5% -> 0% of each run, Pallas kernels for 21% -> 21%
where the time goes in v2:
time: 93.7 us; the launch traced here: 93.4 us
  Pallas kernels  33.1 us (35%)
  waiting for transfers between devices  25.9 us (28%)
  starting transfers between devices  16.9 us (18%)
  blocking collectives  13.4 us (14%)
  local copies, waits for them, and re-layouts  2.51 us (3%)
    pallas_call x2, Pallas kernels, attend(): pl.pallas_call(attend_kernel, grid_spec=pltpu.PrefetchScalarGridSpec(num_...  19.8 us
    all_to_all x1, blocking collectives, body(): blocks = lax.all_to_all(part, 'head', 0, 0)  13.4 us
    all_to_all x1, waiting for transfers between devices, body(): blocks = lax.all_to_all(partial, 'resp', 0, 0, axis_index_groups=SAME_CORE)  12.8 us
    ppermute x1, waiting for transfers between devices, body(): from_across = lax.ppermute(from_below, 'head', UP)  8.86 us
    all_to_all x1, starting transfers between devices, body(): blocks = lax.all_to_all(partial, 'resp', 0, 0, axis_index_groups=SAME_CORE)  8.63 us
    pallas_call x1, Pallas kernels, project(): pl.pallas_call(project_kernel, in_specs=[SMEM] + [vmem] * 9, out_shape=ja...  6.92 us
    ppermute x2, waiting for transfers between devices, body(): got = lax.ppermute(other, 'resp', CORE_SWAP)  4.21 us
    ppermute x1, starting transfers between devices, body(): from_far = lax.ppermute(sent, 'resp', FAR_SWAP)  2.9 us
  transfers between devices with their start and end apart: 8, of which 4 were waited for; matrix products, arithmetic and copies ran while one was open for 0% of the time, Pallas kernels for 21%

profile of v2, /device:TPU:2, one launch (start us, length us, event | category | flops | bytes accessed | tf_op | source)
XLA Modules:
  0.0 93.4 jit_solution(3070823095343630671)
XLA Ops:
  0.6 1.6 %shard_map.227.own_ref = bf16[144,640]{1,0:T(8,128)(2,1)} custom-call(bf16[64,640]{1,0:T(8,128)(2,1)} %upper_ref.1, bf16[64,640]{1,0:T(8,128)(2,1)} %lower_ref.1, bf16[640]{0:T(1024)(128)(2,1)} %upper_gain_ref.1, bf16[640]{0:T(1024)(128)(2,1)} %lower_gain_ref.1), custom_call_target="tpu_custom_call" | custom-call | bytes 400000 | tf_op jit(solution)/shard_map/pallas_call | solution.py:190
  2.3 1.6 %collective-permute-start = (bf16[144,640]{1,0:T(8,128)(2,1)}, bf16[144,640]{1,0:T(8,128)(2,1)S(1)}, u32[]{:S(2)}, u32[]{:S(2)}) collective-permute-start(bf16[144,640]{1,0:T(8,128)(2,1)} %shard_map.227.own_ref), channel_id=1, source_target_pairs={{0,4},{1,5},{2,6},{3,7},{4,0},{5,1},{6,2},{7,3},{8,12},{9,13},{10,... | collective-permute-start | bytes 552968 | tf_op jit(solution)/shard_map/ppermute | solution.py:337
  3.8 9.9 %shard_map.228 = (bf16[128,1024]{1,0:T(8,128)(2,1)}, bf16[128,256]{1,0:T(8,128)(2,1)}, bf16[1024,256]{1,0:T(8,128)(2,1)}, bf16[1024,256]{1,0:T(8,128)(2,1)}) custom-call(s32[1]{0:T(128)} %bitcast.core_ref, bf16[128,1024]{1,0:T(8,128)(2,1)} %q_ref, bf16[128,1024]{1,0:T(8,128)(2,1)} %g_ref.2, bf16[2048,128]{1,0:T(8,128)(2,1)} %k_ref.2, ...), custom_call_target="tpu_custom_call" | custom-call | flops 2852126720 | bytes 4194304 | tf_op jit(solution)/shard_map/pallas_call | solution.py:123
  13.7 0.0 collective-permute-done.near_ref
  13.7 0.1 collective-permute-start.1
  13.8 2.1 %collective-permute-done.1.got_ref = bf16[1024,256]{1,0:T(8,128)(2,1)S(1)} collective-permute-done((bf16[1024,256]{1,0:T(8,128)(2,1)}, bf16[1024,256]{1,0:T(8,128)(2,1)S(1)}, u32[]{:S(2)}, u32[]{:S(2)}) %collective-permute-start.1) | collective-permute-done | bytes 524320 | tf_op jit(solution)/shard_map/ppermute | solution.py:343
  15.9 0.0 copy-done.7
  15.9 0.8 copy-done.1
  16.7 2.4 %shard_map.229 = (bf16[16,32,256]{2,1,0:T(8,128)(2,1)}, bf16[16,32,256]{2,1,0:T(8,128)(2,1)}, bf16[2,144,640]{2,1,0:T(8,128)(2,1)}) custom-call(s32[1]{0:T(128)} %bitcast.1.far_ref, bf16[1024,256]{1,0:T(8,128)(2,1)} %get-tuple-element.29.mine_ref, bf16[1024,256]{1,0:T(8,128)(2,1)} %copy-done.1, bf16[144,640]{1,0:T(8,128)(2,1)} %shard_map.227.own_ref, ...), custom_call_target="tpu_custom_call" | custom-call | bytes 3000000 | tf_op jit(solution)/shard_map/pallas_call | solution.py:219
  19.1 1.5 %collective-permute-start.3 = (bf16[2,144,640]{2,1,0:T(8,128)(2,1)}, bf16[2,144,640]{2,1,0:T(8,128)(2,1)S(1)}, u32[]{:S(2)}, u32[]{:S(2)}) collective-permute-start(bf16[2,144,640]{2,1,0:T(8,128)(2,1)} %get-tuple-element.43.refs_4_), channel_id=1, source_target_pairs={{0,1},{1,2},{2,3},{3,0},{4,5},{5,6},{6,7},{7,4},{8,9},{9,10},{10,1... | collective-permute-start | bytes 1105928 | tf_op jit(solution)/shard_map/ppermute | solution.py:347
  20.6 0.5 collective-permute-start.4
  21.2 2.9 %collective-permute-start.2 = (bf16[16,32,256]{2,1,0:T(8,128)(2,1)}, bf16[16,32,256]{2,1,0:T(8,128)(2,1)S(1)}, u32[]{:S(2)}, u32[]{:S(2)}) collective-permute-start(bf16[16,32,256]{2,1,0:T(8,128)(2,1)} %get-tuple-element.42), channel_id=1, source_target_pairs={{0,128},{8,136},{16,144},{24,152},{32,160},{40,168},{48,176},{56,1... | collective-permute-start | bytes 786440 | tf_op jit(solution)/shard_map/ppermute | solution.py:346
  24.1 9.9 %shard_map.230 = (bf16[128,1024]{1,0:T(8,128)(2,1)}, bf16[128,256]{1,0:T(8,128)(2,1)}, bf16[1024,256]{1,0:T(8,128)(2,1)}, bf16[1024,256]{1,0:T(8,128)(2,1)}) custom-call(s32[1]{0:T(128)} %bitcast.core_ref, bf16[128,1024]{1,0:T(8,128)(2,1)} %q_ref.1, bf16[128,1024]{1,0:T(8,128)(2,1)} %g_ref.3, bf16[2048,128]{1,0:T(8,128)(2,1)} %k_ref.3, ...), custom_call_target="tpu_custom_call" | custom-call | flops 2852126720 | bytes 4194304 | tf_op jit(solution)/shard_map/pallas_call | solution.py:123
  34.0 0.0 collective-permute-done.2.far_ref
  34.0 0.0 collective-permute-done.3.refs_5_
  34.0 0.0 copy-start.3
  34.0 0.0 collective-permute-done.4.refs_6_
  34.0 0.0 copy-start.4
  34.0 0.1 collective-permute-start.5
  34.1 2.1 %collective-permute-done.5.got_ref = bf16[1024,256]{1,0:T(8,128)(2,1)S(1)} collective-permute-done((bf16[1024,256]{1,0:T(8,128)(2,1)}, bf16[1024,256]{1,0:T(8,128)(2,1)S(1)}, u32[]{:S(2)}, u32[]{:S(2)}) %collective-permute-start.5) | collective-permute-done | bytes 524320 | tf_op jit(solution)/shard_map/ppermute | solution.py:356
  36.2 0.0 copy-done.6
  36.2 0.8 copy-done.2
  37.0 2.4 %shard_map.231 = bf16[16,96,256]{2,1,0:T(8,128)(2,1)} custom-call(bf16[16,32,256]{2,1,0:T(8,128)(2,1)} %get-tuple-element.40.kept_ref, bf16[16,32,256]{2,1,0:T(8,128)(2,1)} %copy-done.6, bf16[1024,256]{1,0:T(8,128)(2,1)} %get-tuple-element.45.mine_ref, bf16[1024,256]{1,0:T(8,128)(2,1)} %copy-done.2), custom_call_target="tpu_custom_call" | custom-call | bytes 3000000 | tf_op jit(solution)/shard_map/pallas_call | solution.py:240
  39.5 8.6 %all-to-all-start = ((bf16[16,96,256]{2,1,0:T(8,128)(2,1)}), bf16[16,96,256]{2,1,0:T(8,128)(2,1)S(1)}, u32[]{:S(2)}, u32[]{:S(2)}) async-start(bf16[16,96,256]{2,1,0:T(8,128)(2,1)} %shard_map.231), calls=%async_computation | async-start | bytes 1572864 | tf_op jit(solution)/shard_map/all_to_all | solution.py:359
  48.1 1.6 %collective-permute-start.6 = (bf16[2,144,640]{2,1,0:T(8,128)(2,1)S(1)}, bf16[2,144,640]{2,1,0:T(8,128)(2,1)S(1)}, u32[]{:S(2)}, u32[]{:S(2)}) collective-permute-start(bf16[2,144,640]{2,1,0:T(8,128)(2,1)S(1)} %collective-permute-done.3.refs_5_), channel_id=1, source_target_pairs={{0,1},{1,2},{2,3},{3,0},{4,5},{5,6},{6,7},{7,4},{8,9},{9,10},{10,1... | collective-permute-start | bytes 1105928 | tf_op jit(solution)/shard_map/ppermute | solution.py:358
  49.7 8.9 %collective-permute-done.6.refs_7_ = bf16[2,144,640]{2,1,0:T(8,128)(2,1)S(1)} collective-permute-done((bf16[2,144,640]{2,1,0:T(8,128)(2,1)S(1)}, bf16[2,144,640]{2,1,0:T(8,128)(2,1)S(1)}, u32[]{:S(2)}, u32[]{:S(2)}) %collective-permute-start.6) | collective-permute-done | bytes 368672 | tf_op jit(solution)/shard_map/ppermute | solution.py:358
  58.5 12.8 %all-to-all-done.blocks_ref = bf16[16,96,256]{2,1,0:T(8,128)(2,1)S(1)} async-done(((bf16[16,96,256]{2,1,0:T(8,128)(2,1)}), bf16[16,96,256]{2,1,0:T(8,128)(2,1)S(1)}, u32[]{:S(2)}, u32[]{:S(2)}) %all-to-all-start) | async-done | bytes 786464 | tf_op jit(solution)/shard_map/all_to_all | solution.py:359
  71.4 0.0 copy-done.4
  71.4 0.9 copy-done
  72.3 6.9 %shard_map.232 = bf16[8,64,640]{2,1,0:T(8,128)(2,1)} custom-call(s32[1]{0:T(128)} %bitcast.2.head_ref, bf16[16,96,256]{2,1,0:T(8,128)(2,1)} %copy-done, bf16[5120,128]{1,0:T(8,128)(2,1)} %refs_0_.1, bf16[5120,128]{1,0:T(8,128)(2,1)} %refs_1_.1, bf16[5120,128]{1,0:T(8,128)(2,1)} %refs_2_.1, bf16[5120,128]{1,0:T(8,128)(2,1)} %refs_3_.1, ...), custom_call_target="tpu_custom_call" | custom-call | flops 335544320 | bytes 8000000 | tf_op jit(solution)/shard_map/pallas_call | solution.py:315
  79.2 13.4 %all_to_all.10 = bf16[8,64,640]{2,1,0:T(8,128)(2,1)S(1)} all-to-all(bf16[8,64,640]{2,1,0:T(8,128)(2,1)} %shard_map.232), channel_id=1, replica_groups=mesh['resp'=32,'head'=8] {'head'}, dimensions={0} | all-to-all | bytes 1310720 | tf_op jit(solution)/shard_map/all_to_all | solution.py:366
  92.6 0.7 reduce_sum.12
  (8 shorter events, 0.0 us)
Async XLA Ops:
  2.3 11.5 %collective-permute-start = (bf16[144,640]{1,0:T(8,128)(2,1)}, bf16[144,640]{1,0:T(8,128)(2,1)S(1)}, u32[]{:S(2)}, u32[]{:S(2)}) collective-permute-start(bf16[144,640]{1,0:T(8,128)(2,1)} %shard_map.227.own_ref), channel_id=1, source_target_pairs={{0,4},{1,5},{2,6},{3,7},{4,0},{5,1},{6,2},{7,3},{8,12},{9,13},{10,... | collective-permute-start | bytes 552968 | tf_op jit(solution)/shard_map/ppermute | solution.py:337
  13.7 2.2 %copy-start.7 = (bf16[144,640]{1,0:T(8,128)(2,1)}, bf16[144,640]{1,0:T(8,128)(2,1)S(1)}, u32[]{:S(2)}) copy-start(bf16[144,640]{1,0:T(8,128)(2,1)S(1)} %collective-permute-done.near_ref) | copy-start | bytes 552964
  13.7 2.2 %collective-permute-start.1 = (bf16[1024,256]{1,0:T(8,128)(2,1)}, bf16[1024,256]{1,0:T(8,128)(2,1)S(1)}, u32[]{:S(2)}, u32[]{:S(2)}) collective-permute-start(bf16[1024,256]{1,0:T(8,128)(2,1)} %get-tuple-element.32), channel_id=1, source_target_pairs={{0,8},{8,0},{16,24},{24,16},{32,40},{40,32},{48,56},{56,48},{64,72... | collective-permute-start | bytes 1572872 | tf_op jit(solution)/shard_map/ppermute | solution.py:343
  15.9 0.8 copy-start.1
  19.1 14.8 %collective-permute-start.3 = (bf16[2,144,640]{2,1,0:T(8,128)(2,1)}, bf16[2,144,640]{2,1,0:T(8,128)(2,1)S(1)}, u32[]{:S(2)}, u32[]{:S(2)}) collective-permute-start(bf16[2,144,640]{2,1,0:T(8,128)(2,1)} %get-tuple-element.43.refs_4_), channel_id=1, source_target_pairs={{0,1},{1,2},{2,3},{3,0},{4,5},{5,6},{6,7},{7,4},{8,9},{9,10},{10,1... | collective-permute-start | bytes 1105928 | tf_op jit(solution)/shard_map/ppermute | solution.py:347
  20.6 13.4 %collective-permute-start.4 = (bf16[2,144,640]{2,1,0:T(8,128)(2,1)}, bf16[2,144,640]{2,1,0:T(8,128)(2,1)S(1)}, u32[]{:S(2)}, u32[]{:S(2)}) collective-permute-start(bf16[2,144,640]{2,1,0:T(8,128)(2,1)} %get-tuple-element.43.refs_4_), channel_id=1, source_target_pairs={{0,3},{1,0},{2,1},{3,2},{4,7},{5,4},{6,5},{7,6},{8,11},{9,8},{10,9... | collective-permute-start | bytes 1105928 | tf_op jit(solution)/shard_map/ppermute | solution.py:348
  21.2 12.8 %collective-permute-start.2 = (bf16[16,32,256]{2,1,0:T(8,128)(2,1)}, bf16[16,32,256]{2,1,0:T(8,128)(2,1)S(1)}, u32[]{:S(2)}, u32[]{:S(2)}) collective-permute-start(bf16[16,32,256]{2,1,0:T(8,128)(2,1)} %get-tuple-element.42), channel_id=1, source_target_pairs={{0,128},{8,136},{16,144},{24,152},{32,160},{40,168},{48,176},{56,1... | collective-permute-start | bytes 786440 | tf_op jit(solution)/shard_map/ppermute | solution.py:346
  34.0 2.3 %copy-start.6 = (bf16[16,32,256]{2,1,0:T(8,128)(2,1)}, bf16[16,32,256]{2,1,0:T(8,128)(2,1)S(1)}, u32[]{:S(2)}) copy-start(bf16[16,32,256]{2,1,0:T(8,128)(2,1)S(1)} %collective-permute-done.2.far_ref) | copy-start | bytes 786436
  34.0 37.4 %copy-start.3 = (bf16[2,144,640]{2,1,0:T(8,128)(2,1)}, bf16[2,144,640]{2,1,0:T(8,128)(2,1)S(1)}, u32[]{:S(2)}) copy-start(bf16[2,144,640]{2,1,0:T(8,128)(2,1)S(1)} %collective-permute-done.3.refs_5_) | copy-start | bytes 1105924
  34.0 37.4 %copy-start.4 = (bf16[2,144,640]{2,1,0:T(8,128)(2,1)}, bf16[2,144,640]{2,1,0:T(8,128)(2,1)S(1)}, u32[]{:S(2)}) copy-start(bf16[2,144,640]{2,1,0:T(8,128)(2,1)S(1)} %collective-permute-done.4.refs_6_) | copy-start | bytes 1105924
  34.0 2.2 %collective-permute-start.5 = (bf16[1024,256]{1,0:T(8,128)(2,1)}, bf16[1024,256]{1,0:T(8,128)(2,1)S(1)}, u32[]{:S(2)}, u32[]{:S(2)}) collective-permute-start(bf16[1024,256]{1,0:T(8,128)(2,1)} %get-tuple-element.46), channel_id=1, source_target_pairs={{0,8},{8,0},{16,24},{24,16},{32,40},{40,32},{48,56},{56,48},{64,72... | collective-permute-start | bytes 1572872 | tf_op jit(solution)/shard_map/ppermute | solution.py:356
  36.2 0.8 copy-start.2
  39.5 31.9 %all-to-all-start = ((bf16[16,96,256]{2,1,0:T(8,128)(2,1)}), bf16[16,96,256]{2,1,0:T(8,128)(2,1)S(1)}, u32[]{:S(2)}, u32[]{:S(2)}) async-start(bf16[16,96,256]{2,1,0:T(8,128)(2,1)} %shard_map.231), calls=%async_computation | async-start | bytes 1572864 | tf_op jit(solution)/shard_map/all_to_all | solution.py:359
  48.1 10.4 %collective-permute-start.6 = (bf16[2,144,640]{2,1,0:T(8,128)(2,1)S(1)}, bf16[2,144,640]{2,1,0:T(8,128)(2,1)S(1)}, u32[]{:S(2)}, u32[]{:S(2)}) collective-permute-start(bf16[2,144,640]{2,1,0:T(8,128)(2,1)S(1)} %collective-permute-done.3.refs_5_), channel_id=1, source_target_pairs={{0,1},{1,2},{2,3},{3,0},{4,5},{5,6},{6,7},{7,4},{8,9},{9,10},{10,1... | collective-permute-start | bytes 1105928 | tf_op jit(solution)/shard_map/ppermute | solution.py:358
  58.5 12.8 %copy-start.5 = (bf16[2,144,640]{2,1,0:T(8,128)(2,1)}, bf16[2,144,640]{2,1,0:T(8,128)(2,1)S(1)}, u32[]{:S(2)}) copy-start(bf16[2,144,640]{2,1,0:T(8,128)(2,1)S(1)} %collective-permute-done.6.refs_7_) | copy-start | bytes 1105924
  71.4 0.9 copy-start

commit v3 on v2

v3 whole, which is shorter than its diff:
```python
import functools
import jax
import jax.numpy as jnp
from jax import lax
from jax.experimental import pallas as pl
from jax.experimental.pallas import tpu as pltpu
from jax.sharding import PartitionSpec as P

HEAD = 128
C = 64
NT = (((1,), (1,)), ((), ()))
LAG = 6
TN = (((0,), (0,)), ((), ()))


def attend_kernel(core_ref, q_hbm, g_hbm, k_hbm, v_hbm, sk_hbm, sv_hbm, slopes_hbm, span_hbm,
                  mine_hbm, other_hbm, scores, dots, key_sums, value_sums,
                  q_ref, g_ref, k_ref, v_ref, sk_ref, sv_ref, sems,
                  slopes_ref, span_ref, mine_ref, other_ref, out_sems):
    copies = [
        pltpu.make_async_copy(source, target, sems.at[i])
        for i, (source, target) in enumerate((
            (q_hbm, q_ref), (k_hbm, k_ref), (sk_hbm, sk_ref), (g_hbm, g_ref), (v_hbm, v_ref),
            (sv_hbm, sv_ref),
        ))
    ]
    for copy in copies:
        copy.start()
    for copy in copies[:2]:
        copy.wait()
    tokens = q_ref.shape[0]
    prompt = k_ref.shape[0]
    group = 2
    pair = group * tokens
    pairs = q_ref.shape[1] // (group * HEAD)
    scale = HEAD ** -0.5
    factor = scale * 1.4426950408889634
    chunk = 2 * C
    count = prompt // chunk + 1
    parts = [slice(j * chunk, (j + 1) * chunk) for j in range(count)]
    even = core_ref[0] == 0

    def rows_of(ref, span, j):
        return ref[parts[j], :] if j < count - 1 else span[...]

    def stacked(ref, p):
        heads = [ref[:, h * HEAD:(h + 1) * HEAD] for h in range(group * p, group * p + group)]
        return jnp.concatenate(heads, axis=0)

    def first_pass(p, state):
        query = stacked(q_ref, p)
        grad = None if p == 0 else stacked(g_ref, p)
        tops = []
        totals = []
        deltas = []
        for j in range(count):
            block = lax.dot_general(
                rows_of(k_ref, sk_ref, j), query, NT, preferred_element_type=jnp.float32
            )
            if j == count - 1:
                u = lax.broadcasted_iota(jnp.int32, block.shape, 0)
                t = lax.rem(lax.broadcasted_iota(jnp.int32, block.shape, 1), tokens)
                block = jnp.where((lax.div(u, C) == lax.div(t, C)) & (u <= t), block, -1e30)
            top = jnp.max(block, axis=0, keepdims=True)
            block = jnp.exp2((block - top) * factor)
            scores[p, parts[j], :] = block
            if grad is None:
                for copy in copies[2:]:
                    copy.wait()
                grad = stacked(g_ref, p)
            dot = lax.dot_general(
                rows_of(v_ref, sv_ref, j), grad, NT, preferred_element_type=jnp.float32
            )
            dots[p, parts[j], :] = dot
            tops.append(top)
            totals.append(jnp.sum(block, axis=0, keepdims=True))
            deltas.append(jnp.sum(block * dot, axis=0, keepdims=True))
            yield
        tops = jnp.concatenate(tops, axis=0)
        weigh = jnp.exp2((tops - jnp.max(tops, axis=0, keepdims=True)) * factor)
        total = jnp.sum(weigh * jnp.concatenate(totals, axis=0), axis=0, keepdims=True)
        weigh = weigh / total
        delta = jnp.sum(weigh * jnp.concatenate(deltas, axis=0), axis=0, keepdims=True)
        state[p] = (query, grad, weigh, delta)

    def second_pass(p, state):
        query, grad, weigh, delta = state.pop(p)
        for j in range(count):
            weight = scores[p, parts[j], :] * weigh[j:j + 1, :]
            slope = (weight * (dots[p, parts[j], :] - delta)).astype(jnp.bfloat16)
            weight = weight.astype(jnp.bfloat16)
            slopes_ref[p, parts[j], :] = slope
            key_sum = jnp.dot(slope, query, preferred_element_type=jnp.float32)
            value_sum = jnp.dot(weight, grad, preferred_element_type=jnp.float32)
            if p > 0:
                key_sum = key_sum + key_sums[parts[j], :]
                value_sum = value_sum + value_sums[parts[j], :]
            if p < pairs - 1:
                key_sums[parts[j], :] = key_sum
                value_sums[parts[j], :] = value_sum
            else:
                both = jnp.concatenate([key_sum * scale, value_sum], axis=1)
                if j == count - 1:
                    span_ref[...] = both.astype(jnp.bfloat16)
                    send(span_ref, span_hbm)
                else:
                    half = slice(j * C, (j + 1) * C)
                    mine_ref[half, :] = jnp.where(even, both[:C], both[C:]).astype(jnp.bfloat16)
                    other_ref[half, :] = jnp.where(even, both[C:], both[:C]).astype(jnp.bfloat16)
                    if j % 4 == 3:
                        ready = slice((j - 3) * C, (j + 1) * C)
                        send(other_ref.at[ready, :], other_hbm.at[ready, :])
                        send(mine_ref.at[ready, :], mine_hbm.at[ready, :])
            yield
        send(slopes_ref.at[p], slopes_hbm.at[p])

    outs = []

    def send(source, target):
        copy = pltpu.make_async_copy(source, target, out_sems.at[len(outs)])
        copy.start()
        outs.append(copy)

    state = {}

    def chained(one):
        for p in range(pairs):
            yield from one(p, state)

    first = chained(first_pass)
    second = chained(second_pass)
    for ahead in range(count + LAG):
        next(first)
    for unused in second:
        next(first, None)
    for copy in outs:
        copy.wait()


def attend(core, q, k, v, sk, sv, g):
    tokens = q.shape[0]
    heads = q.shape[1] // HEAD
    prompt = k.shape[0]
    rows = prompt + tokens

    def whole(*shape):
        return pl.BlockSpec(shape, lambda i, core: (0, 0))

    paired = whole(tokens, heads * HEAD)
    return pl.pallas_call(
        attend_kernel,
        grid_spec=pltpu.PrefetchScalarGridSpec(
            num_scalar_prefetch=1,
            grid=(1,),
            in_specs=[
                pl.BlockSpec(memory_space=pl.ANY)
            ] * 6,
            out_specs=[pl.BlockSpec(memory_space=pl.ANY)] * 4,
            scratch_shapes=[
                pltpu.VMEM((heads // 2, rows, 2 * tokens), jnp.float32),
                pltpu.VMEM((heads // 2, rows, 2 * tokens), jnp.float32),
                pltpu.VMEM((rows, HEAD), jnp.float32),
                pltpu.VMEM((rows, HEAD), jnp.float32),
                pltpu.VMEM(q.shape, jnp.bfloat16),
                pltpu.VMEM(g.shape, jnp.bfloat16),
                pltpu.VMEM(k.shape, jnp.bfloat16),
                pltpu.VMEM(v.shape, jnp.bfloat16),
                pltpu.VMEM(sk.shape, jnp.bfloat16),
                pltpu.VMEM(sv.shape, jnp.bfloat16),
                pltpu.SemaphoreType.DMA((6,)),
                pltpu.VMEM((heads // 2, rows, 2 * tokens), jnp.bfloat16),
                pltpu.VMEM((tokens, 2 * HEAD), jnp.bfloat16),
                pltpu.VMEM((prompt // 2, 2 * HEAD), jnp.bfloat16),
                pltpu.VMEM((prompt // 2, 2 * HEAD), jnp.bfloat16),
                pltpu.SemaphoreType.DMA((13,)),
            ],
        ),
        out_shape=[
            jax.ShapeDtypeStruct((heads // 2, rows, 2 * tokens), jnp.bfloat16),
            jax.ShapeDtypeStruct((tokens, 2 * HEAD), jnp.bfloat16),
            jax.ShapeDtypeStruct((prompt // 2, 2 * HEAD), jnp.bfloat16),
            jax.ShapeDtypeStruct((prompt // 2, 2 * HEAD), jnp.bfloat16),
        ],
        compiler_params=pltpu.CompilerParams(vmem_limit_bytes=62 * 1024 * 1024),
        cost_estimate=pl.CostEstimate(
            flops=10 * rows * heads * tokens * HEAD,
            bytes_accessed=4 * 1024 * 1024,
            transcendentals=rows * heads * tokens,
        ),
    )(core, q, g, k, v, sk, sv)


def query_kernel(slopes_ref, k_ref, sk_ref, dq_ref):
    prompt = k_ref.shape[0]
    tokens = dq_ref.shape[0]
    sums = lax.dot_general(
        slopes_ref[0, :prompt, :], k_ref[...], TN, preferred_element_type=jnp.float32
    ) + lax.dot_general(
        slopes_ref[0, prompt:, :], sk_ref[...], TN, preferred_element_type=jnp.float32
    )
    sums = (sums * HEAD ** -0.5).astype(jnp.bfloat16)
    dq_ref[:, :HEAD] = sums[:tokens]
    dq_ref[:, HEAD:] = sums[tokens:]


def query_grads(slopes, k, sk):
    pairs, rows, width = slopes.shape
    tokens = sk.shape[0]
    return pl.pallas_call(
        query_kernel,
        grid=(pairs,),
        in_specs=[
            pl.BlockSpec((1, rows, width), lambda i: (i, 0, 0)),
            pl.BlockSpec(k.shape, lambda i: (0, 0)),
            pl.BlockSpec(sk.shape, lambda i: (0, 0)),
        ],
        out_specs=pl.BlockSpec((tokens, width), lambda i: (0, i)),
        out_shape=jax.ShapeDtypeStruct((tokens, pairs * width), jnp.bfloat16),
        compiler_params=pltpu.CompilerParams(vmem_limit_bytes=62 * 1024 * 1024),
        cost_estimate=pl.CostEstimate(
            flops=2 * pairs * rows * width * HEAD,
            bytes_accessed=6 * 1024 * 1024,
            transcendentals=0,
        ),
    )(slopes, k, sk)


D = 5120
epsilon = 1e-06
RESP = 32
HEADS = 8
CORE_SWAP = [(i, i ^ 1) for i in range(RESP)]
FAR_SWAP = [(i, i ^ 16) for i in range(RESP)]
SAME_CORE = [[2 * i + c for i in range(RESP // 2)] for c in range(2)]
NEAR_SWAP = [(i, i ^ 4) for i in range(HEADS)]
UP = [(i, i // 4 * 4 + (i + 1) % 4) for i in range(HEADS)]
DOWN = [(i, i // 4 * 4 + (i + 3) % 4) for i in range(HEADS)]
EXTRA = 16
SMEM = pl.BlockSpec(memory_space=pltpu.SMEM)
BIG_VMEM = pltpu.CompilerParams(vmem_limit_bytes=62 * 1024 * 1024)


def cost(read, flops=0):
    return pl.CostEstimate(flops=flops, bytes_accessed=read, transcendentals=0)


def pack_kernel(upper_ref, lower_ref, upper_gain_ref, lower_gain_ref, out_ref):
    rows, width = upper_ref.shape
    place = lax.broadcasted_iota(jnp.int32, (EXTRA, width), 0)
    upper_gain = upper_gain_ref[...].astype(jnp.float32).reshape(1, width)
    lower_gain = lower_gain_ref[...].astype(jnp.float32).reshape(1, width)
    gains = jnp.where(place == 0, upper_gain, jnp.where(place == 1, lower_gain, 0.0))
    out_ref[:rows, :] = upper_ref[...]
    out_ref[rows : 2 * rows, :] = lower_ref[...]
    out_ref[2 * rows :, :] = gains.astype(jnp.bfloat16)


def pack(upper_input, lower_input, upper_gain, lower_gain):
    rows, width = upper_input.shape
    return pl.pallas_call(
        pack_kernel,
        out_shape=jax.ShapeDtypeStruct((2 * rows + EXTRA, width), jnp.bfloat16),
        compiler_params=BIG_VMEM,
        cost_estimate=cost(400000),
    )(upper_input, lower_input, upper_gain, lower_gain)


def split(far, mine, got):
    total = mine.astype(jnp.float32) + got.astype(jnp.float32)
    total = total.astype(jnp.bfloat16).reshape(RESP // 2, 2, -1, mine.shape[1])
    low = far == 0
    kept = jnp.where(low, total[:, 0], total[:, 1])
    sent = jnp.where(low, total[:, 1], total[:, 0])
    return kept, sent


def join(kept, far, mine, got):
    upper = (kept.astype(jnp.float32) + far.astype(jnp.float32)).astype(jnp.bfloat16)
    lower = (mine.astype(jnp.float32) + got.astype(jnp.float32)).astype(jnp.bfloat16)
    return jnp.concatenate([upper, lower.reshape(RESP // 2, -1, mine.shape[1])], axis=1)


def project_kernel(head_ref, blocks_ref, *refs):
    piece_refs = refs[:8]
    weight_hbm = refs[8:12]
    out_ref, weights_ref, scaled, sems = refs[12:]
    count, rows, width = out_ref.shape
    half = rows // 2
    sources = blocks_ref.shape[0]
    copies = [
        pltpu.make_async_copy(
            source, weights_ref.at[w // 2, :, pl.ds(w % 2 * HEAD, HEAD)], sems.at[w]
        )
        for w, source in enumerate(weight_hbm)
    ]
    for copy in copies:
        copy.start()

    def total(first, last, part):
        summed = blocks_ref[first, part, :].astype(jnp.float32)
        for i in range(first + 1, last):
            summed = summed + blocks_ref[i, part, :].astype(jnp.float32)
        return summed.astype(jnp.bfloat16)

    upper = jnp.concatenate(
        [
            total(0, sources // 2, slice(0, half)),
            total(sources // 2, sources, slice(0, half)),
        ],
        axis=0,
    )
    lower = total(0, sources, slice(half, 3 * half))
    near = lax.div(head_ref[0], 4)
    across = lax.rem(head_ref[0], 4)
    owners = []
    for shift in (0, 3, 1, 2):
        for side in (near, 1 - near):
            owners.append(side * 4 + lax.rem(across + shift, 4))
    inverses = []
    shrinks = []
    groups = width // 128

    def folded(values):
        return sum(values[:, g * 128 : (g + 1) * 128] for g in range(groups))

    for layer, rounded in enumerate((upper, lower)):
        place = slice(layer * rows, (layer + 1) * rows)
        squares = jnp.zeros((rows, 128), jnp.float32)
        sums = jnp.zeros((rows, 128), jnp.float32)
        for piece_ref in piece_refs:
            hidden = piece_ref[place, :].astype(jnp.float32)
            squares = squares + folded(hidden * hidden)
        for copy in copies[2 * layer : 2 * layer + 2]:
            copy.wait()
        for i, (piece_ref, owner) in enumerate(zip(piece_refs, owners)):
            columns = pl.ds(pl.multiple_of(owner * width, 128), width)
            gains = piece_ref[2 * rows :, :].astype(jnp.float32)
            projected = lax.dot_general(
                rounded, weights_ref[layer, columns, :], NT, preferred_element_type=jnp.float32
            )
            one = projected * gains[layer : layer + 1]
            scaled[layer, i] = one
            sums = sums + folded(one * piece_ref[place, :].astype(jnp.float32))
        squares = jnp.sum(squares, axis=1, keepdims=True)
        sums = jnp.sum(sums, axis=1, keepdims=True)
        inverse = lax.rsqrt(squares / D + epsilon)
        inverses.append(inverse)
        shrinks.append(inverse * inverse * inverse * sums / D)
    for i, (piece_ref, owner) in enumerate(zip(piece_refs, owners)):
        part = jnp.zeros((rows, width), jnp.float32)
        for layer in range(2):
            hidden = piece_ref[layer * rows : (layer + 1) * rows, :].astype(jnp.float32)
            part = part + inverses[layer] * scaled[layer, i] - shrinks[layer] * hidden
        out_ref[owner] = part.astype(jnp.bfloat16)


def project(head, blocks, weights, pieces):
    rows = blocks.shape[1] // 3 * 2
    width = pieces[0].shape[1]
    vmem = pl.BlockSpec(memory_space=pltpu.VMEM)
    return pl.pallas_call(
        project_kernel,
        in_specs=[SMEM] + [vmem] * 9 + [pl.BlockSpec(memory_space=pl.ANY)] * 4,
        out_specs=vmem,
        out_shape=jax.ShapeDtypeStruct((HEADS, rows, width), jnp.bfloat16),
        scratch_shapes=[
            pltpu.VMEM((2, D, 2 * HEAD), jnp.bfloat16),
            pltpu.VMEM((2, HEADS, rows, width), jnp.float32),
            pltpu.SemaphoreType.DMA((4,)),
        ],
        compiler_params=pltpu.CompilerParams(vmem_limit_bytes=58 * 1024 * 1024),
        cost_estimate=cost(8000000, 8 * rows * D * HEAD),
    )(head, blocks, *pieces, *weights)


def body(
    upper_input, upper_gain, upper_key_weight, upper_value_weight, upper_prompt_keys,
    upper_prompt_values, upper_queries, upper_span_keys, upper_span_values, upper_out_grad,
    lower_input, lower_gain, lower_key_weight, lower_value_weight, lower_prompt_keys,
    lower_prompt_values, lower_queries, lower_span_keys, lower_span_values, lower_out_grad,
):
    place = lax.axis_index("resp").astype(jnp.int32)
    core = lax.rem(place, 2).reshape(1)
    far = lax.div(place, 16)
    head = lax.axis_index("head").astype(jnp.int32).reshape(1)
    own = pack(upper_input, lower_input, upper_gain, lower_gain)
    own, upper_queries = lax.optimization_barrier((own, upper_queries))
    near = lax.ppermute(own, "head", NEAR_SWAP)
    upper_slopes, upper_span, mine, other = attend(
        core, upper_queries, upper_prompt_keys, upper_prompt_values, upper_span_keys,
        upper_span_values, upper_out_grad,
    )
    other, near = lax.optimization_barrier((other, near))
    got = lax.ppermute(other, "resp", CORE_SWAP)
    kept, sent = split(far, mine, got)
    sent, own, near, lower_queries = lax.optimization_barrier((sent, own, near, lower_queries))
    from_far = lax.ppermute(sent, "resp", FAR_SWAP)
    below = [lax.ppermute(one, "head", UP) for one in (own, near)]
    lower_slopes, lower_span, mine, other = attend(
        core, lower_queries, lower_prompt_keys, lower_prompt_values, lower_span_keys,
        lower_span_values, lower_out_grad,
    )
    other, from_far, below = lax.optimization_barrier((other, from_far, below))
    got = lax.ppermute(other, "resp", CORE_SWAP)
    partial = join(kept, from_far, mine, got)
    partial, own, near, below, upper_slopes = lax.optimization_barrier(
        (partial, own, near, below, upper_slopes)
    )
    across = [lax.ppermute(one, "head", UP) for one in below]
    above = [lax.ppermute(one, "head", DOWN) for one in (own, near)]
    blocks = lax.all_to_all(partial, "resp", 0, 0, axis_index_groups=SAME_CORE)
    upper_query = query_grads(upper_slopes, upper_prompt_keys, upper_span_keys)
    blocks, upper_query = lax.optimization_barrier((blocks, upper_query))
    part = project(
        head,
        blocks,
        (upper_key_weight, upper_value_weight, lower_key_weight, lower_value_weight),
        (own, near, *below, *above, *across),
    )
    part, lower_slopes = lax.optimization_barrier((part, lower_slopes))
    blocks = lax.all_to_all(part, "head", 0, 0)
    lower_query = query_grads(lower_slopes, lower_prompt_keys, lower_span_keys)
    prompt_grads = jnp.sum(blocks.astype(jnp.float32), axis=0).astype(jnp.bfloat16)
    return (upper_query, lower_query, upper_span, lower_span, prompt_grads)


def solution(mesh):
    layer = (
        P("resp", "head"), P("head"), P(None, "head"), P(None, "head"), P(None, "head"),
        P(None, "head"), P("resp", "head"), P("resp", "head"), P("resp", "head"), P("resp", "head"),
    )
    return jax.shard_map(
        body,
        mesh=mesh,
        in_specs=layer + layer,
        out_specs=(P("resp", "head"),) * 5,
        check_vma=False,
    )
```

time: 93.7 us -> 89 us (0.950)
  blocking collectives: 13.4 us -> 0 us
  starting transfers between devices: 16.9 us -> 24.5 us
  waiting for transfers between devices: 25.9 us -> 21.6 us
  other arithmetic: 0.73 us -> 4.21 us
  Pallas kernels: 33.1 us -> 36.2 us
  local copies, waits for them, and re-layouts: 2.51 us -> 1.03 us
    all_to_all x1 -> x0, blocking collectives: 13.4 us -> none  [body(): blocks = lax.all_to_all(part, 'head', 0, 0)]
    ppermute x3 -> x6, waiting for transfers between devices: 8.87 us -> 0.02 us  [the longest x2 0.01 us: body(): below = [lax.ppermute(one, 'head', UP) for one in (own, near)]]
    pallas_call x3, Pallas kernels: 11.7 us -> 16.6 us  [the longest x2 9.9 us: query_grads(): pl.pallas_call(query_kernel, grid=(pairs,), in_specs=[pl.BlockSpec((1, ro...]
    all_to_all x0 -> x1, starting transfers between devices: none -> 4.29 us  [body(): blocks = lax.all_to_all(part, 'head', 0, 0)]
    all_to_all x0 -> x1, waiting for transfers between devices: none -> 3.34 us  [body(): blocks = lax.all_to_all(part, 'head', 0, 0)]
    ppermute x3 -> x6, starting transfers between devices: 3.6 us -> 6.89 us  [the longest x2 2.77 us: body(): below = [lax.ppermute(one, 'head', UP) for one in (own, near)]]
    convert_element_type x0 -> x3, other arithmetic: none -> 2.47 us  [the longest x1 1.17 us: split(): total = total.astype(jnp.bfloat16).reshape(RESP // 2, 2, -1, mine.shape[1])]
    pallas_call x2, Pallas kernels: 19.8 us -> 18 us  [attend(): pl.pallas_call(attend_kernel, grid_spec=pltpu.PrefetchScalarGridSpec(num_...]
  transfers between devices with their start and end apart: 8 -> 12, of which waited for: 4 -> 4; matrix products, arithmetic and copies ran while one was open for 0% -> 0% of each run, Pallas kernels for 21% -> 32%
where the time goes in v3:
time: 89 us; the launch traced here: 88.3 us
  Pallas kernels  36.2 us (41%)
  starting transfers between devices  24.5 us (28%)
  waiting for transfers between devices  21.6 us (24%)
  other arithmetic  4.21 us (5%)
  local copies, waits for them, and re-layouts  1.03 us (1%)
    pallas_call x2, Pallas kernels, attend(): pl.pallas_call(attend_kernel, grid_spec=pltpu.PrefetchScalarGridSpec(num_...  18 us
    all_to_all x1, waiting for transfers between devices, body(): blocks = lax.all_to_all(partial, 'resp', 0, 0, axis_index_groups=SAME_CORE)  14.2 us
    pallas_call x2, Pallas kernels, query_grads(): pl.pallas_call(query_kernel, grid=(pairs,), in_specs=[pl.BlockSpec((1, ro...  9.9 us
    all_to_all x1, starting transfers between devices, body(): blocks = lax.all_to_all(partial, 'resp', 0, 0, axis_index_groups=SAME_CORE)  8.64 us
    pallas_call x1, Pallas kernels, project(): pl.pallas_call(project_kernel, in_specs=[SMEM] + [vmem] * 9 + [pl.BlockSp...  6.66 us
    all_to_all x1, starting transfers between devices, body(): blocks = lax.all_to_all(part, 'head', 0, 0)  4.29 us
    ppermute x2, waiting for transfers between devices, body(): got = lax.ppermute(other, 'resp', CORE_SWAP)  4.08 us
    all_to_all x1, waiting for transfers between devices, body(): blocks = lax.all_to_all(part, 'head', 0, 0)  3.34 us
  transfers between devices with their start and end apart: 12, of which 4 were waited for; matrix products, arithmetic and copies ran while one was open for 0% of the time, Pallas kernels for 32%

profile of v3, /device:TPU:2, one launch (start us, length us, event | category | flops | bytes accessed | tf_op | source)
XLA Modules:
  0.0 88.3 jit_solution(7477572656237549269)
XLA Ops:
  0.6 1.6 %shard_map.227.refs_0_ = bf16[144,640]{1,0:T(8,128)(2,1)} custom-call(bf16[64,640]{1,0:T(8,128)(2,1)} %upper_ref.1, bf16[64,640]{1,0:T(8,128)(2,1)} %lower_ref.1, bf16[640]{0:T(1024)(128)(2,1)} %upper_gain_ref.1, bf16[640]{0:T(1024)(128)(2,1)} %lower_gain_ref.1), custom_call_target="tpu_custom_call" | custom-call | bytes 400000 | tf_op jit(solution)/shard_map/pallas_call | solution.py:260
  2.3 1.6 %collective-permute-start = (bf16[144,640]{1,0:T(8,128)(2,1)}, bf16[144,640]{1,0:T(8,128)(2,1)S(1)}, u32[]{:S(2)}, u32[]{:S(2)}) collective-permute-start(bf16[144,640]{1,0:T(8,128)(2,1)} %shard_map.227.refs_0_), channel_id=1, source_target_pairs={{0,4},{1,5},{2,6},{3,7},{4,0},{5,1},{6,2},{7,3},{8,12},{9,13},{10,... | collective-permute-start | bytes 552968 | tf_op jit(solution)/shard_map/ppermute | solution.py:388
  3.8 9.0 %shard_map.228 = (bf16[4,2176,256]{2,1,0:T(8,128)(2,1)}, bf16[128,256]{1,0:T(8,128)(2,1)}, bf16[1024,256]{1,0:T(8,128)(2,1)}, bf16[1024,256]{1,0:T(8,128)(2,1)}) custom-call(s32[1]{0:T(128)} %bitcast.core_ref, bf16[128,1024]{1,0:T(8,128)(2,1)} %q_hbm, bf16[128,1024]{1,0:T(8,128)(2,1)} %g_hbm.2, bf16[2048,128]{1,0:T(8,128)(2,1)} %k_ref.2, ...), custom_call_target="tpu_custom_call" | custom-call | flops 2852126720 | bytes 4194304 | tf_op jit(solution)/shard_map/pallas_call | solution.py:150
  12.9 0.0 copy-start.1
  12.9 0.0 collective-permute-done.refs_1_
  12.9 0.1 collective-permute-start.1
  13.0 2.1 %collective-permute-done.1 = bf16[1024,256]{1,0:T(8,128)(2,1)S(1)} collective-permute-done((bf16[1024,256]{1,0:T(8,128)(2,1)}, bf16[1024,256]{1,0:T(8,128)(2,1)S(1)}, u32[]{:S(2)}, u32[]{:S(2)}) %collective-permute-start.1) | collective-permute-done | bytes 524320 | tf_op jit(solution)/shard_map/ppermute | solution.py:394
  15.1 1.2 %add_convert_fusion.1 = bf16[1024,256]{1,0:T(8,128)(2,1)S(1)} fusion(bf16[1024,256]{1,0:T(8,128)(2,1)S(1)} %collective-permute-done.1, bf16[1024,256]{1,0:T(8,128)(2,1)} %get-tuple-element.36), kind=kLoop, calls=%fused_computation.1 | loop fusion | flops 1048576 | bytes 1572864 | tf_op jit(solution)/shard_map/convert_element_type | solution.py:270
  16.4 1.6 %collective-permute-start.3 = (bf16[144,640]{1,0:T(8,128)(2,1)S(1)}, bf16[144,640]{1,0:T(8,128)(2,1)S(1)}, u32[]{:S(2)}, u32[]{:S(2)}) collective-permute-start(bf16[144,640]{1,0:T(8,128)(2,1)S(1)} %copy-done.1), channel_id=1, source_target_pairs={{0,1},{1,2},{2,3},{3,0},{4,5},{5,6},{6,7},{7,4},{8,9},{9,10},{10,1... | collective-permute-start | bytes 552968 | tf_op jit(solution)/shard_map/ppermute | solution.py:398
  17.9 1.2 %collective-permute-start.4 = (bf16[144,640]{1,0:T(8,128)(2,1)S(1)}, bf16[144,640]{1,0:T(8,128)(2,1)S(1)}, u32[]{:S(2)}, u32[]{:S(2)}) collective-permute-start(bf16[144,640]{1,0:T(8,128)(2,1)S(1)} %collective-permute-done.refs_1_), channel_id=1, source_target_pairs={{0,1},{1,2},{2,3},{3,0},{4,5},{5,6},{6,7},{7,4},{8,9},{9,10},{10,1... | collective-permute-start | bytes 552968 | tf_op jit(solution)/shard_map/ppermute | solution.py:398
  19.1 2.9 %collective-permute-start.2 = (bf16[16,32,256]{2,1,0:T(8,128)(2,1)S(1)}, bf16[16,32,256]{2,1,0:T(8,128)(2,1)S(1)}, u32[]{:S(2)}, u32[]{:S(2)}) collective-permute-start(bf16[16,32,256]{2,1,0:T(8,128)(2,1)S(1)} %select_bitcast_fusion), channel_id=1, source_target_pairs={{0,128},{8,136},{16,144},{24,152},{32,160},{40,168},{48,176},{56,1... | collective-permute-start | bytes 786440 | tf_op jit(solution)/shard_map/ppermute | solution.py:397
  22.0 8.9 %shard_map.229 = (bf16[4,2176,256]{2,1,0:T(8,128)(2,1)}, bf16[128,256]{1,0:T(8,128)(2,1)}, bf16[1024,256]{1,0:T(8,128)(2,1)}, bf16[1024,256]{1,0:T(8,128)(2,1)}) custom-call(s32[1]{0:T(128)} %bitcast.core_ref, bf16[128,1024]{1,0:T(8,128)(2,1)} %q_hbm.1, bf16[128,1024]{1,0:T(8,128)(2,1)} %g_hbm.3, bf16[2048,128]{1,0:T(8,128)(2,1)} %k_ref.3, ...), custom_call_target="tpu_custom_call" | custom-call | flops 2852126720 | bytes 4194304 | tf_op jit(solution)/shard_map/pallas_call | solution.py:150
  31.0 0.1 collective-permute-start.5
  31.1 0.1 fusion
  31.3 2.0 %collective-permute-done.5 = bf16[1024,256]{1,0:T(8,128)(2,1)S(1)} collective-permute-done((bf16[1024,256]{1,0:T(8,128)(2,1)}, bf16[1024,256]{1,0:T(8,128)(2,1)S(1)}, u32[]{:S(2)}, u32[]{:S(2)}) %collective-permute-start.5) | collective-permute-done | bytes 524320 | tf_op jit(solution)/shard_map/ppermute | solution.py:404
  33.2 1.2 %add_convert_fusion = bf16[1024,256]{1,0:T(8,128)(2,1)S(1)} fusion(bf16[1024,256]{1,0:T(8,128)(2,1)S(1)} %collective-permute-done.5, bf16[1024,256]{1,0:T(8,128)(2,1)} %get-tuple-element.47), kind=kLoop, calls=%fused_computation | loop fusion | flops 1048576 | bytes 1572864 | tf_op jit(solution)/shard_map/convert_element_type | solution.py:279
  34.4 1.0 %pad_maximum_fusion = bf16[16,96,256]{2,1,0:T(8,128)(2,1)} fusion(bf16[16,64,256]{2,1,0:T(8,128)(2,1)S(1)} %bitcast.23, bf16[16,32,256]{2,1,0:T(8,128)(2,1)S(1)} %fusion), kind=kLoop, calls=%fused_computation.2 | loop fusion | flops 1572864 | bytes 1572864 | tf_op jit(solution)/shard_map/concatenate | solution.py:280
  35.4 8.6 %all-to-all-start = ((bf16[16,96,256]{2,1,0:T(8,128)(2,1)}), bf16[16,96,256]{2,1,0:T(8,128)(2,1)S(1)}, u32[]{:S(2)}, u32[]{:S(2)}) async-start(bf16[16,96,256]{2,1,0:T(8,128)(2,1)} %pad_maximum_fusion), calls=%async_computation | async-start | bytes 1572864 | tf_op jit(solution)/shard_map/all_to_all | solution.py:411
  44.0 0.9 %collective-permute-start.6 = (bf16[144,640]{1,0:T(8,128)(2,1)S(1)}, bf16[144,640]{1,0:T(8,128)(2,1)S(1)}, u32[]{:S(2)}, u32[]{:S(2)}) collective-permute-start(bf16[144,640]{1,0:T(8,128)(2,1)S(1)} %copy-done.1), channel_id=1, source_target_pairs={{0,3},{1,0},{2,1},{3,2},{4,7},{5,4},{6,5},{7,6},{8,11},{9,8},{10,9... | collective-permute-start | bytes 552968 | tf_op jit(solution)/shard_map/ppermute | solution.py:410
  45.0 1.7 %collective-permute-start.7 = (bf16[144,640]{1,0:T(8,128)(2,1)S(1)}, bf16[144,640]{1,0:T(8,128)(2,1)S(1)}, u32[]{:S(2)}, u32[]{:S(2)}) collective-permute-start(bf16[144,640]{1,0:T(8,128)(2,1)S(1)} %collective-permute-done.refs_1_), channel_id=1, source_target_pairs={{0,3},{1,0},{2,1},{3,2},{4,7},{5,4},{6,5},{7,6},{8,11},{9,8},{10,9... | collective-permute-start | bytes 552968 | tf_op jit(solution)/shard_map/ppermute | solution.py:410
  46.7 0.3 collective-permute-start.8
  47.0 1.2 %collective-permute-start.9 = (bf16[144,640]{1,0:T(8,128)(2,1)S(1)}, bf16[144,640]{1,0:T(8,128)(2,1)}, u32[]{:S(2)}, u32[]{:S(2)}) collective-permute-start(bf16[144,640]{1,0:T(8,128)(2,1)S(1)} %collective-permute-done.4.refs_3_), channel_id=1, source_target_pairs={{0,1},{1,2},{2,3},{3,0},{4,5},{5,6},{6,7},{7,4},{8,9},{9,10},{10,1... | collective-permute-start | bytes 552968 | tf_op jit(solution)/shard_map/ppermute | solution.py:409
  48.2 4.9 %shard_map.230 = bf16[128,1024]{1,0:T(8,128)(2,1)} custom-call(bf16[4,2176,256]{2,1,0:T(8,128)(2,1)} %get-tuple-element.53.slopes_ref, bf16[2048,128]{1,0:T(8,128)(2,1)} %k_ref.2, bf16[128,128]{1,0:T(8,128)(2,1)} %sk_ref.2), custom_call_target="tpu_custom_call" | custom-call | flops 570425344 | bytes 6291456 | tf_op jit(solution)/shard_map/pallas_call | solution.py:209
  53.1 14.2 %all-to-all-done.blocks_ref = bf16[16,96,256]{2,1,0:T(8,128)(2,1)S(1)} async-done(((bf16[16,96,256]{2,1,0:T(8,128)(2,1)}), bf16[16,96,256]{2,1,0:T(8,128)(2,1)S(1)}, u32[]{:S(2)}, u32[]{:S(2)}) %all-to-all-start) | async-done | bytes 786464 | tf_op jit(solution)/shard_map/all_to_all | solution.py:411
  67.4 0.8 copy-done
  68.2 0.1 copy-done.5
  68.3 0.1 copy-done.6
  68.4 6.7 %shard_map.231 = bf16[8,64,640]{2,1,0:T(8,128)(2,1)} custom-call(s32[1]{0:T(128)} %bitcast.5.head_ref, bf16[16,96,256]{2,1,0:T(8,128)(2,1)} %copy-done, bf16[144,640]{1,0:T(8,128)(2,1)} %shard_map.227.refs_0_, bf16[144,640]{1,0:T(8,128)(2,1)} %copy-done.2, bf16[144,640]{1,0:T(8,128)(2,1)} %copy-done.3, bf16[144,640]{1,0:T(8,128)(2,1)} %copy-done.4, ...), custom_call_target="tpu_custom_call" | custom-call | flops 335544320 | bytes 8000000 | tf_op jit(solution)/shard_map/pallas_call | solution.py:361
  75.0 4.3 %all-to-all-start.1 = ((bf16[8,64,640]{2,1,0:T(8,128)(2,1)}), bf16[8,64,640]{2,1,0:T(8,128)(2,1)S(1)}, u32[]{:S(2)}, u32[]{:S(2)}) async-start(bf16[8,64,640]{2,1,0:T(8,128)(2,1)} %shard_map.231), calls=%async_computation.1 | async-start | bytes 1310720 | tf_op jit(solution)/shard_map/all_to_all | solution.py:421
  79.3 4.9 %shard_map.232 = bf16[128,1024]{1,0:T(8,128)(2,1)} custom-call(bf16[4,2176,256]{2,1,0:T(8,128)(2,1)} %get-tuple-element.61.slopes_ref, bf16[2048,128]{1,0:T(8,128)(2,1)} %k_ref.3, bf16[128,128]{1,0:T(8,128)(2,1)} %sk_ref.3), custom_call_target="tpu_custom_call" | custom-call | flops 570425344 | bytes 6291456 | tf_op jit(solution)/shard_map/pallas_call | solution.py:209
  84.3 3.3 %all-to-all-done.1 = bf16[8,64,640]{2,1,0:T(8,128)(2,1)S(1)} async-done(((bf16[8,64,640]{2,1,0:T(8,128)(2,1)}), bf16[8,64,640]{2,1,0:T(8,128)(2,1)S(1)}, u32[]{:S(2)}, u32[]{:S(2)}) %all-to-all-start.1) | async-done | bytes 655392 | tf_op jit(solution)/shard_map/all_to_all | solution.py:421
  87.6 0.7 reduce_sum.12
  (18 shorter events, 0.1 us)
Async XLA Ops:
  2.3 10.6 %collective-permute-start = (bf16[144,640]{1,0:T(8,128)(2,1)}, bf16[144,640]{1,0:T(8,128)(2,1)S(1)}, u32[]{:S(2)}, u32[]{:S(2)}) collective-permute-start(bf16[144,640]{1,0:T(8,128)(2,1)} %shard_map.227.refs_0_), channel_id=1, source_target_pairs={{0,4},{1,5},{2,6},{3,7},{4,0},{5,1},{6,2},{7,3},{8,12},{9,13},{10,... | collective-permute-start | bytes 552968 | tf_op jit(solution)/shard_map/ppermute | solution.py:388
  12.9 3.5 %copy-start.1 = (bf16[144,640]{1,0:T(8,128)(2,1)S(1)}, bf16[144,640]{1,0:T(8,128)(2,1)}, u32[]{:S(2)}) copy-start(bf16[144,640]{1,0:T(8,128)(2,1)} %shard_map.227.refs_0_) | copy-start | bytes 552964
  12.9 32.0 %copy-start.2 = (bf16[144,640]{1,0:T(8,128)(2,1)}, bf16[144,640]{1,0:T(8,128)(2,1)S(1)}, u32[]{:S(2)}) copy-start(bf16[144,640]{1,0:T(8,128)(2,1)S(1)} %collective-permute-done.refs_1_) | copy-start | bytes 552964
  12.9 2.2 %collective-permute-start.1 = (bf16[1024,256]{1,0:T(8,128)(2,1)}, bf16[1024,256]{1,0:T(8,128)(2,1)S(1)}, u32[]{:S(2)}, u32[]{:S(2)}) collective-permute-start(bf16[1024,256]{1,0:T(8,128)(2,1)} %get-tuple-element.39), channel_id=1, source_target_pairs={{0,8},{8,0},{16,24},{24,16},{32,40},{40,32},{48,56},{56,48},{64,72... | collective-permute-start | bytes 1572872 | tf_op jit(solution)/shard_map/ppermute | solution.py:394
  16.4 14.6 %collective-permute-start.3 = (bf16[144,640]{1,0:T(8,128)(2,1)S(1)}, bf16[144,640]{1,0:T(8,128)(2,1)S(1)}, u32[]{:S(2)}, u32[]{:S(2)}) collective-permute-start(bf16[144,640]{1,0:T(8,128)(2,1)S(1)} %copy-done.1), channel_id=1, source_target_pairs={{0,1},{1,2},{2,3},{3,0},{4,5},{5,6},{6,7},{7,4},{8,9},{9,10},{10,1... | collective-permute-start | bytes 552968 | tf_op jit(solution)/shard_map/ppermute | solution.py:398
  17.9 13.1 %collective-permute-start.4 = (bf16[144,640]{1,0:T(8,128)(2,1)S(1)}, bf16[144,640]{1,0:T(8,128)(2,1)S(1)}, u32[]{:S(2)}, u32[]{:S(2)}) collective-permute-start(bf16[144,640]{1,0:T(8,128)(2,1)S(1)} %collective-permute-done.refs_1_), channel_id=1, source_target_pairs={{0,1},{1,2},{2,3},{3,0},{4,5},{5,6},{6,7},{7,4},{8,9},{9,10},{10,1... | collective-permute-start | bytes 552968 | tf_op jit(solution)/shard_map/ppermute | solution.py:398
  19.1 11.9 %collective-permute-start.2 = (bf16[16,32,256]{2,1,0:T(8,128)(2,1)S(1)}, bf16[16,32,256]{2,1,0:T(8,128)(2,1)S(1)}, u32[]{:S(2)}, u32[]{:S(2)}) collective-permute-start(bf16[16,32,256]{2,1,0:T(8,128)(2,1)S(1)} %select_bitcast_fusion), channel_id=1, source_target_pairs={{0,128},{8,136},{16,144},{24,152},{32,160},{40,168},{48,176},{56,1... | collective-permute-start | bytes 786440 | tf_op jit(solution)/shard_map/ppermute | solution.py:397
  31.0 15.7 %copy-start.3 = (bf16[144,640]{1,0:T(8,128)(2,1)}, bf16[144,640]{1,0:T(8,128)(2,1)S(1)}, u32[]{:S(2)}) copy-start(bf16[144,640]{1,0:T(8,128)(2,1)S(1)} %collective-permute-done.3.refs_2_) | copy-start | bytes 552964
  31.0 16.0 %copy-start.4 = (bf16[144,640]{1,0:T(8,128)(2,1)}, bf16[144,640]{1,0:T(8,128)(2,1)S(1)}, u32[]{:S(2)}) copy-start(bf16[144,640]{1,0:T(8,128)(2,1)S(1)} %collective-permute-done.4.refs_3_) | copy-start | bytes 552964
  31.0 2.2 %collective-permute-start.5 = (bf16[1024,256]{1,0:T(8,128)(2,1)}, bf16[1024,256]{1,0:T(8,128)(2,1)S(1)}, u32[]{:S(2)}, u32[]{:S(2)}) collective-permute-start(bf16[1024,256]{1,0:T(8,128)(2,1)} %get-tuple-element.48), channel_id=1, source_target_pairs={{0,8},{8,0},{16,24},{24,16},{32,40},{40,32},{48,56},{56,48},{64,72... | collective-permute-start | bytes 1572872 | tf_op jit(solution)/shard_map/ppermute | solution.py:404
  35.4 31.9 %all-to-all-start = ((bf16[16,96,256]{2,1,0:T(8,128)(2,1)}), bf16[16,96,256]{2,1,0:T(8,128)(2,1)S(1)}, u32[]{:S(2)}, u32[]{:S(2)}) async-start(bf16[16,96,256]{2,1,0:T(8,128)(2,1)} %pad_maximum_fusion), calls=%async_computation | async-start | bytes 1572864 | tf_op jit(solution)/shard_map/all_to_all | solution.py:411
  44.0 23.3 %collective-permute-start.6 = (bf16[144,640]{1,0:T(8,128)(2,1)S(1)}, bf16[144,640]{1,0:T(8,128)(2,1)S(1)}, u32[]{:S(2)}, u32[]{:S(2)}) collective-permute-start(bf16[144,640]{1,0:T(8,128)(2,1)S(1)} %copy-done.1), channel_id=1, source_target_pairs={{0,3},{1,0},{2,1},{3,2},{4,7},{5,4},{6,5},{7,6},{8,11},{9,8},{10,9... | collective-permute-start | bytes 552968 | tf_op jit(solution)/shard_map/ppermute | solution.py:410
  45.0 22.4 %collective-permute-start.7 = (bf16[144,640]{1,0:T(8,128)(2,1)S(1)}, bf16[144,640]{1,0:T(8,128)(2,1)S(1)}, u32[]{:S(2)}, u32[]{:S(2)}) collective-permute-start(bf16[144,640]{1,0:T(8,128)(2,1)S(1)} %collective-permute-done.refs_1_), channel_id=1, source_target_pairs={{0,3},{1,0},{2,1},{3,2},{4,7},{5,4},{6,5},{7,6},{8,11},{9,8},{10,9... | collective-permute-start | bytes 552968 | tf_op jit(solution)/shard_map/ppermute | solution.py:410
  46.7 20.6 %collective-permute-start.8 = (bf16[144,640]{1,0:T(8,128)(2,1)S(1)}, bf16[144,640]{1,0:T(8,128)(2,1)}, u32[]{:S(2)}, u32[]{:S(2)}) collective-permute-start(bf16[144,640]{1,0:T(8,128)(2,1)S(1)} %collective-permute-done.3.refs_2_), channel_id=1, source_target_pairs={{0,1},{1,2},{2,3},{3,0},{4,5},{5,6},{6,7},{7,4},{8,9},{9,10},{10,1... | collective-permute-start | bytes 552968 | tf_op jit(solution)/shard_map/ppermute | solution.py:409
  47.0 20.4 %collective-permute-start.9 = (bf16[144,640]{1,0:T(8,128)(2,1)S(1)}, bf16[144,640]{1,0:T(8,128)(2,1)}, u32[]{:S(2)}, u32[]{:S(2)}) collective-permute-start(bf16[144,640]{1,0:T(8,128)(2,1)S(1)} %collective-permute-done.4.refs_3_), channel_id=1, source_target_pairs={{0,1},{1,2},{2,3},{3,0},{4,5},{5,6},{6,7},{7,4},{8,9},{9,10},{10,1... | collective-permute-start | bytes 552968 | tf_op jit(solution)/shard_map/ppermute | solution.py:409
  67.3 0.9 %copy-start = (bf16[16,96,256]{2,1,0:T(8,128)(2,1)}, bf16[16,96,256]{2,1,0:T(8,128)(2,1)S(1)}, u32[]{:S(2)}) copy-start(bf16[16,96,256]{2,1,0:T(8,128)(2,1)S(1)} %all-to-all-done.blocks_ref) | copy-start | bytes 2359300
  67.3 1.0 %copy-start.5 = (bf16[144,640]{1,0:T(8,128)(2,1)}, bf16[144,640]{1,0:T(8,128)(2,1)S(1)}, u32[]{:S(2)}) copy-start(bf16[144,640]{1,0:T(8,128)(2,1)S(1)} %collective-permute-done.6.refs_4_) | copy-start | bytes 552964
  67.3 1.0 %copy-start.6 = (bf16[144,640]{1,0:T(8,128)(2,1)}, bf16[144,640]{1,0:T(8,128)(2,1)S(1)}, u32[]{:S(2)}) copy-start(bf16[144,640]{1,0:T(8,128)(2,1)S(1)} %collective-permute-done.7.refs_5_) | copy-start | bytes 552964
  75.0 12.6 %all-to-all-start.1 = ((bf16[8,64,640]{2,1,0:T(8,128)(2,1)}), bf16[8,64,640]{2,1,0:T(8,128)(2,1)S(1)}, u32[]{:S(2)}, u32[]{:S(2)}) async-start(bf16[8,64,640]{2,1,0:T(8,128)(2,1)} %shard_map.231), calls=%async_computation.1 | async-start | bytes 1310720 | tf_op jit(solution)/shard_map/all_to_all | solution.py:421

commit v4 on v3

--- a/solution.py
+++ b/solution.py
@@ -235,6 +235,7 @@
 NEAR_SWAP = [(i, i ^ 4) for i in range(HEADS)]
 UP = [(i, i // 4 * 4 + (i + 1) % 4) for i in range(HEADS)]
 DOWN = [(i, i // 4 * 4 + (i + 3) % 4) for i in range(HEADS)]
+ACROSS = [(i, i ^ 2) for i in range(HEADS)]
 EXTRA = 16
 SMEM = pl.BlockSpec(memory_space=pltpu.SMEM)
 BIG_VMEM = pltpu.CompilerParams(vmem_limit_bytes=62 * 1024 * 1024)
@@ -383,30 +384,27 @@
     core = lax.rem(place, 2).reshape(1)
     far = lax.div(place, 16)
     head = lax.axis_index("head").astype(jnp.int32).reshape(1)
-    own = pack(upper_input, lower_input, upper_gain, lower_gain)
-    own, upper_queries = lax.optimization_barrier((own, upper_queries))
-    near = lax.ppermute(own, "head", NEAR_SWAP)
     upper_slopes, upper_span, mine, other = attend(
         core, upper_queries, upper_prompt_keys, upper_prompt_values, upper_span_keys,
         upper_span_values, upper_out_grad,
     )
-    other, near = lax.optimization_barrier((other, near))
+    other, upper_input = lax.optimization_barrier((other, upper_input))
     got = lax.ppermute(other, "resp", CORE_SWAP)
+    own = pack(upper_input, lower_input, upper_gain, lower_gain)
     kept, sent = split(far, mine, got)
-    sent, own, near, lower_queries = lax.optimization_barrier((sent, own, near, lower_queries))
+    sent, own, lower_queries = lax.optimization_barrier((sent, own, lower_queries))
     from_far = lax.ppermute(sent, "resp", FAR_SWAP)
-    below = [lax.ppermute(one, "head", UP) for one in (own, near)]
+    near = lax.ppermute(own, "head", NEAR_SWAP)
     lower_slopes, lower_span, mine, other = attend(
         core, lower_queries, lower_prompt_keys, lower_prompt_values, lower_span_keys,
         lower_span_values, lower_out_grad,
     )
-    other, from_far, below = lax.optimization_barrier((other, from_far, below))
+    other, from_far, near = lax.optimization_barrier((other, from_far, near))
     got = lax.ppermute(other, "resp", CORE_SWAP)
     partial = join(kept, from_far, mine, got)
-    partial, own, near, below, upper_slopes = lax.optimization_barrier(
-        (partial, own, near, below, upper_slopes)
-    )
-    across = [lax.ppermute(one, "head", UP) for one in below]
+    partial, own, near, upper_slopes = lax.optimization_barrier((partial, own, near, upper_slopes))
+    below = [lax.ppermute(one, "head", UP) for one in (own, near)]
+    across = [lax.ppermute(one, "head", ACROSS) for one in (own, near)]
     above = [lax.ppermute(one, "head", DOWN) for one in (own, near)]
     blocks = lax.all_to_all(partial, "resp", 0, 0, axis_index_groups=SAME_CORE)
     upper_query = query_grads(upper_slopes, upper_prompt_keys, upper_span_keys)

time: 89 us -> 86.9 us (0.976)
  waiting for transfers between devices: 21.6 us -> 17 us
  starting transfers between devices: 24.5 us -> 27.1 us
    all_to_all x1, waiting for transfers between devices: 14.2 us -> 8.58 us  [body(): blocks = lax.all_to_all(partial, 'resp', 0, 0, axis_index_groups=SAME_CORE)]
    ppermute x2, starting transfers between devices: 1.48 us -> 4.25 us  [body(): across = [lax.ppermute(one, 'head', ACROSS) for one in (own, near)]]
    ppermute x2, waiting for transfers between devices: 4.08 us -> 2.45 us  [body(): got = lax.ppermute(other, 'resp', CORE_SWAP)]
    ppermute x2, starting transfers between devices: 2.64 us -> 1.07 us  [body(): above = [lax.ppermute(one, 'head', DOWN) for one in (own, near)]]
    ppermute x2, waiting for transfers between devices: 0.01 us -> 1.35 us  [body(): below = [lax.ppermute(one, 'head', UP) for one in (own, near)]]
    ppermute x1, waiting for transfers between devices: 0.01 us -> 1.31 us  [body(): near = lax.ppermute(own, 'head', NEAR_SWAP)]
    all_to_all x1, starting transfers between devices: 8.64 us -> 9.85 us  [body(): blocks = lax.all_to_all(partial, 'resp', 0, 0, axis_index_groups=SAME_CORE)]
    ppermute x1, starting transfers between devices: 1.58 us -> 0.68 us  [body(): near = lax.ppermute(own, 'head', NEAR_SWAP)]
  transfers between devices with their start and end apart: 12 -> 12, of which waited for: 4 -> 6; matrix products, arithmetic and copies ran while one was open for 0% -> 0% of each run, Pallas kernels for 32% -> 24%
where the time goes in v4:
time: 86.9 us; the launch traced here: 86.3 us
  Pallas kernels  36.1 us (42%)
  starting transfers between devices  27.1 us (31%)
  waiting for transfers between devices  17 us (20%)
  other arithmetic  4.21 us (5%)
  local copies, waits for them, and re-layouts  1.08 us (1%)
    pallas_call x2, Pallas kernels, attend(): pl.pallas_call(attend_kernel, grid_spec=pltpu.PrefetchScalarGridSpec(num_...  18 us
    pallas_call x2, Pallas kernels, query_grads(): pl.pallas_call(query_kernel, grid=(pairs,), in_specs=[pl.BlockSpec((1, ro...  9.9 us
    all_to_all x1, starting transfers between devices, body(): blocks = lax.all_to_all(partial, 'resp', 0, 0, axis_index_groups=SAME_CORE)  9.85 us
    all_to_all x1, waiting for transfers between devices, body(): blocks = lax.all_to_all(partial, 'resp', 0, 0, axis_index_groups=SAME_CORE)  8.58 us
    pallas_call x1, Pallas kernels, project(): pl.pallas_call(project_kernel, in_specs=[SMEM] + [vmem] * 9 + [pl.BlockSp...  6.62 us
    all_to_all x1, starting transfers between devices, body(): blocks = lax.all_to_all(part, 'head', 0, 0)  4.85 us
    ppermute x2, starting transfers between devices, body(): across = [lax.ppermute(one, 'head', ACROSS) for one in (own, near)]  4.25 us
    ppermute x1, starting transfers between devices, body(): from_far = lax.ppermute(sent, 'resp', FAR_SWAP)  3.28 us
  transfers between devices with their start and end apart: 12, of which 6 were waited for; matrix products, arithmetic and copies ran while one was open for 0% of the time, Pallas kernels for 24%

profile of v4, /device:TPU:2, one launch (start us, length us, event | category | flops | bytes accessed | tf_op | source)
XLA Modules:
  0.0 86.3 jit_solution(4535182908667639864)
XLA Ops:
  0.6 9.0 %shard_map.227 = (bf16[4,2176,256]{2,1,0:T(8,128)(2,1)}, bf16[128,256]{1,0:T(8,128)(2,1)}, bf16[1024,256]{1,0:T(8,128)(2,1)}, bf16[1024,256]{1,0:T(8,128)(2,1)}) custom-call(s32[1]{0:T(128)} %bitcast.core_ref, bf16[128,1024]{1,0:T(8,128)(2,1)} %q_hbm.1, bf16[128,1024]{1,0:T(8,128)(2,1)} %g_hbm.2, bf16[2048,128]{1,0:T(8,128)(2,1)} %k_ref.2, ...), custom_call_target="tpu_custom_call" | custom-call | flops 2852126720 | bytes 4194304 | tf_op jit(solution)/shard_map/pallas_call | solution.py:150
  9.7 0.1 collective-permute-start
  9.8 1.6 %shard_map.228.refs_0_ = bf16[144,640]{1,0:T(8,128)(2,1)} custom-call(bf16[64,640]{1,0:T(8,128)(2,1)} %upper_ref, bf16[64,640]{1,0:T(8,128)(2,1)} %lower_ref.1, bf16[640]{0:T(1024)(128)(2,1)} %upper_gain_ref.1, bf16[640]{0:T(1024)(128)(2,1)} %lower_gain_ref.1), custom_call_target="tpu_custom_call" | custom-call | bytes 400000 | tf_op jit(solution)/shard_map/pallas_call | solution.py:261
  11.4 0.5 collective-permute-done
  11.9 1.2 %add_convert_fusion.1 = bf16[1024,256]{1,0:T(8,128)(2,1)S(1)} fusion(bf16[1024,256]{1,0:T(8,128)(2,1)S(1)} %collective-permute-done, bf16[1024,256]{1,0:T(8,128)(2,1)} %get-tuple-element.29), kind=kLoop, calls=%fused_computation.1 | loop fusion | flops 1048576 | bytes 1572864 | tf_op jit(solution)/shard_map/convert_element_type | solution.py:271
  13.1 3.3 %collective-permute-start.1 = (bf16[16,32,256]{2,1,0:T(8,128)(2,1)S(1)}, bf16[16,32,256]{2,1,0:T(8,128)(2,1)S(1)}, u32[]{:S(2)}, u32[]{:S(2)}) collective-permute-start(bf16[16,32,256]{2,1,0:T(8,128)(2,1)S(1)} %select_bitcast_fusion), channel_id=1, source_target_pairs={{0,128},{8,136},{16,144},{24,152},{32,160},{40,168},{48,176},{56,1... | collective-permute-start | bytes 786440 | tf_op jit(solution)/shard_map/ppermute | solution.py:396
  16.4 0.7 collective-permute-start.2
  17.1 8.9 %shard_map.229 = (bf16[4,2176,256]{2,1,0:T(8,128)(2,1)}, bf16[128,256]{1,0:T(8,128)(2,1)}, bf16[1024,256]{1,0:T(8,128)(2,1)}, bf16[1024,256]{1,0:T(8,128)(2,1)}) custom-call(s32[1]{0:T(128)} %bitcast.core_ref, bf16[128,1024]{1,0:T(8,128)(2,1)} %q_hbm.2, bf16[128,1024]{1,0:T(8,128)(2,1)} %g_hbm.3, bf16[2048,128]{1,0:T(8,128)(2,1)} %k_ref.3, ...), custom_call_target="tpu_custom_call" | custom-call | flops 2852126720 | bytes 4194304 | tf_op jit(solution)/shard_map/pallas_call | solution.py:150
  26.1 1.3 %collective-permute-done.2.refs_1_ = bf16[144,640]{1,0:T(8,128)(2,1)S(1)} collective-permute-done((bf16[144,640]{1,0:T(8,128)(2,1)S(1)}, bf16[144,640]{1,0:T(8,128)(2,1)S(1)}, u32[]{:S(2)}, u32[]{:S(2)}) %collective-permute-start.2) | collective-permute-done | bytes 184352 | tf_op jit(solution)/shard_map/ppermute | solution.py:397
  27.4 0.1 fusion
  27.5 2.0 %collective-permute-done.3 = bf16[1024,256]{1,0:T(8,128)(2,1)S(1)} collective-permute-done((bf16[1024,256]{1,0:T(8,128)(2,1)}, bf16[1024,256]{1,0:T(8,128)(2,1)S(1)}, u32[]{:S(2)}, u32[]{:S(2)}) %collective-permute-start.3) | collective-permute-done | bytes 524320 | tf_op jit(solution)/shard_map/ppermute | solution.py:403
  29.5 1.2 %add_convert_fusion = bf16[1024,256]{1,0:T(8,128)(2,1)S(1)} fusion(bf16[1024,256]{1,0:T(8,128)(2,1)S(1)} %collective-permute-done.3, bf16[1024,256]{1,0:T(8,128)(2,1)} %get-tuple-element.38), kind=kLoop, calls=%fused_computation | loop fusion | flops 1048576 | bytes 1572864 | tf_op jit(solution)/shard_map/convert_element_type | solution.py:280
  30.7 1.0 %pad_maximum_fusion = bf16[16,96,256]{2,1,0:T(8,128)(2,1)} fusion(bf16[16,64,256]{2,1,0:T(8,128)(2,1)S(1)} %bitcast.23, bf16[16,32,256]{2,1,0:T(8,128)(2,1)S(1)} %fusion), kind=kLoop, calls=%fused_computation.2 | loop fusion | flops 1572864 | bytes 1572864 | tf_op jit(solution)/shard_map/concatenate | solution.py:281
  31.6 9.8 %all-to-all-start = ((bf16[16,96,256]{2,1,0:T(8,128)(2,1)}), bf16[16,96,256]{2,1,0:T(8,128)(2,1)S(1)}, u32[]{:S(2)}, u32[]{:S(2)}) async-start(bf16[16,96,256]{2,1,0:T(8,128)(2,1)} %pad_maximum_fusion), calls=%async_computation | async-start | bytes 1572864 | tf_op jit(solution)/shard_map/all_to_all | solution.py:409
  41.5 1.6 %collective-permute-start.4 = (bf16[144,640]{1,0:T(8,128)(2,1)S(1)}, bf16[144,640]{1,0:T(8,128)(2,1)S(1)}, u32[]{:S(2)}, u32[]{:S(2)}) collective-permute-start(bf16[144,640]{1,0:T(8,128)(2,1)S(1)} %copy-done.1), channel_id=1, source_target_pairs={{0,1},{1,2},{2,3},{3,0},{4,5},{5,6},{6,7},{7,4},{8,9},{9,10},{10,1... | collective-permute-start | bytes 552968 | tf_op jit(solution)/shard_map/ppermute | solution.py:406
  43.1 0.5 collective-permute-start.6
  43.6 1.5 %collective-permute-start.5 = (bf16[144,640]{1,0:T(8,128)(2,1)S(1)}, bf16[144,640]{1,0:T(8,128)(2,1)S(1)}, u32[]{:S(2)}, u32[]{:S(2)}) collective-permute-start(bf16[144,640]{1,0:T(8,128)(2,1)S(1)} %collective-permute-done.2.refs_1_), channel_id=1, source_target_pairs={{0,1},{1,2},{2,3},{3,0},{4,5},{5,6},{6,7},{7,4},{8,9},{9,10},{10,1... | collective-permute-start | bytes 552968 | tf_op jit(solution)/shard_map/ppermute | solution.py:406
  45.1 0.5 collective-permute-start.7
  45.6 2.1 %collective-permute-start.8 = (bf16[144,640]{1,0:T(8,128)(2,1)S(1)}, bf16[144,640]{1,0:T(8,128)(2,1)}, u32[]{:S(2)}, u32[]{:S(2)}) collective-permute-start(bf16[144,640]{1,0:T(8,128)(2,1)S(1)} %copy-done.1), channel_id=1, source_target_pairs={{0,2},{1,3},{2,0},{3,1},{4,6},{5,7},{6,4},{7,5},{8,10},{9,11},{10,... | collective-permute-start | bytes 552968 | tf_op jit(solution)/shard_map/ppermute | solution.py:407
  47.7 1.3 %collective-permute-done.4.refs_2_ = bf16[144,640]{1,0:T(8,128)(2,1)S(1)} collective-permute-done((bf16[144,640]{1,0:T(8,128)(2,1)S(1)}, bf16[144,640]{1,0:T(8,128)(2,1)S(1)}, u32[]{:S(2)}, u32[]{:S(2)}) %collective-permute-start.4) | collective-permute-done | bytes 184352 | tf_op jit(solution)/shard_map/ppermute | solution.py:406
  49.1 2.1 %collective-permute-start.9 = (bf16[144,640]{1,0:T(8,128)(2,1)S(1)}, bf16[144,640]{1,0:T(8,128)(2,1)}, u32[]{:S(2)}, u32[]{:S(2)}) collective-permute-start(bf16[144,640]{1,0:T(8,128)(2,1)S(1)} %collective-permute-done.2.refs_1_), channel_id=1, source_target_pairs={{0,2},{1,3},{2,0},{3,1},{4,6},{5,7},{6,4},{7,5},{8,10},{9,11},{10,... | collective-permute-start | bytes 552968 | tf_op jit(solution)/shard_map/ppermute | solution.py:407
  51.2 4.9 %shard_map.230 = bf16[128,1024]{1,0:T(8,128)(2,1)} custom-call(bf16[4,2176,256]{2,1,0:T(8,128)(2,1)} %get-tuple-element.43.slopes_ref, bf16[2048,128]{1,0:T(8,128)(2,1)} %k_ref.2, bf16[128,128]{1,0:T(8,128)(2,1)} %sk_ref.2), custom_call_target="tpu_custom_call" | custom-call | flops 570425344 | bytes 6291456 | tf_op jit(solution)/shard_map/pallas_call | solution.py:209
  56.2 8.6 %all-to-all-done.blocks_ref = bf16[16,96,256]{2,1,0:T(8,128)(2,1)S(1)} async-done(((bf16[16,96,256]{2,1,0:T(8,128)(2,1)}), bf16[16,96,256]{2,1,0:T(8,128)(2,1)S(1)}, u32[]{:S(2)}, u32[]{:S(2)}) %all-to-all-start) | async-done | bytes 786464 | tf_op jit(solution)/shard_map/all_to_all | solution.py:409
  64.8 0.8 copy-done
  65.6 0.1 copy-done.5
  65.7 0.1 copy-done.4
  65.8 0.1 copy-done.6
  65.9 6.6 %shard_map.231 = bf16[8,64,640]{2,1,0:T(8,128)(2,1)} custom-call(s32[1]{0:T(128)} %bitcast.5.head_ref, bf16[16,96,256]{2,1,0:T(8,128)(2,1)} %copy-done, bf16[144,640]{1,0:T(8,128)(2,1)} %shard_map.228.refs_0_, bf16[144,640]{1,0:T(8,128)(2,1)} %copy-done.2, bf16[144,640]{1,0:T(8,128)(2,1)} %copy-done.3, bf16[144,640]{1,0:T(8,128)(2,1)} %copy-done.5, ...), custom_call_target="tpu_custom_call" | custom-call | flops 335544320 | bytes 8000000 | tf_op jit(solution)/shard_map/pallas_call | solution.py:362
  72.5 4.8 %all-to-all-start.1 = ((bf16[8,64,640]{2,1,0:T(8,128)(2,1)}), bf16[8,64,640]{2,1,0:T(8,128)(2,1)S(1)}, u32[]{:S(2)}, u32[]{:S(2)}) async-start(bf16[8,64,640]{2,1,0:T(8,128)(2,1)} %shard_map.231), calls=%async_computation.1 | async-start | bytes 1310720 | tf_op jit(solution)/shard_map/all_to_all | solution.py:419
  77.4 4.9 %shard_map.232 = bf16[128,1024]{1,0:T(8,128)(2,1)} custom-call(bf16[4,2176,256]{2,1,0:T(8,128)(2,1)} %get-tuple-element.49.slopes_ref, bf16[2048,128]{1,0:T(8,128)(2,1)} %k_ref.3, bf16[128,128]{1,0:T(8,128)(2,1)} %sk_ref.3), custom_call_target="tpu_custom_call" | custom-call | flops 570425344 | bytes 6291456 | tf_op jit(solution)/shard_map/pallas_call | solution.py:209
  82.3 3.3 %all-to-all-done.1 = bf16[8,64,640]{2,1,0:T(8,128)(2,1)S(1)} async-done(((bf16[8,64,640]{2,1,0:T(8,128)(2,1)}), bf16[8,64,640]{2,1,0:T(8,128)(2,1)S(1)}, u32[]{:S(2)}, u32[]{:S(2)}) %all-to-all-start.1) | async-done | bytes 655392 | tf_op jit(solution)/shard_map/all_to_all | solution.py:419
  85.6 0.7 reduce_sum.12
  (18 shorter events, 0.1 us)
Async XLA Ops:
  9.7 2.2 %collective-permute-start = (bf16[1024,256]{1,0:T(8,128)(2,1)}, bf16[1024,256]{1,0:T(8,128)(2,1)S(1)}, u32[]{:S(2)}, u32[]{:S(2)}) collective-permute-start(bf16[1024,256]{1,0:T(8,128)(2,1)} %get-tuple-element.31), channel_id=1, source_target_pairs={{0,8},{8,0},{16,24},{24,16},{32,40},{40,32},{48,56},{56,48},{64,72... | collective-permute-start | bytes 1572872 | tf_op jit(solution)/shard_map/ppermute | solution.py:392
  11.4 5.0 %copy-start.1 = (bf16[144,640]{1,0:T(8,128)(2,1)S(1)}, bf16[144,640]{1,0:T(8,128)(2,1)}, u32[]{:S(2)}) copy-start(bf16[144,640]{1,0:T(8,128)(2,1)} %shard_map.228.refs_0_) | copy-start | bytes 552964
  13.1 14.2 %collective-permute-start.1 = (bf16[16,32,256]{2,1,0:T(8,128)(2,1)S(1)}, bf16[16,32,256]{2,1,0:T(8,128)(2,1)S(1)}, u32[]{:S(2)}, u32[]{:S(2)}) collective-permute-start(bf16[16,32,256]{2,1,0:T(8,128)(2,1)S(1)} %select_bitcast_fusion), channel_id=1, source_target_pairs={{0,128},{8,136},{16,144},{24,152},{32,160},{40,168},{48,176},{56,1... | collective-permute-start | bytes 786440 | tf_op jit(solution)/shard_map/ppermute | solution.py:396
  16.4 10.9 %collective-permute-start.2 = (bf16[144,640]{1,0:T(8,128)(2,1)S(1)}, bf16[144,640]{1,0:T(8,128)(2,1)S(1)}, u32[]{:S(2)}, u32[]{:S(2)}) collective-permute-start(bf16[144,640]{1,0:T(8,128)(2,1)S(1)} %copy-done.1), channel_id=1, source_target_pairs={{0,4},{1,5},{2,6},{3,7},{4,0},{5,1},{6,2},{7,3},{8,12},{9,13},{10,... | collective-permute-start | bytes 552968 | tf_op jit(solution)/shard_map/ppermute | solution.py:397
  27.4 21.7 %copy-start.2 = (bf16[144,640]{1,0:T(8,128)(2,1)}, bf16[144,640]{1,0:T(8,128)(2,1)S(1)}, u32[]{:S(2)}) copy-start(bf16[144,640]{1,0:T(8,128)(2,1)S(1)} %collective-permute-done.2.refs_1_) | copy-start | bytes 552964
  27.4 2.1 %collective-permute-start.3 = (bf16[1024,256]{1,0:T(8,128)(2,1)}, bf16[1024,256]{1,0:T(8,128)(2,1)S(1)}, u32[]{:S(2)}, u32[]{:S(2)}) collective-permute-start(bf16[1024,256]{1,0:T(8,128)(2,1)} %get-tuple-element.39), channel_id=1, source_target_pairs={{0,8},{8,0},{16,24},{24,16},{32,40},{40,32},{48,56},{56,48},{64,72... | collective-permute-start | bytes 1572872 | tf_op jit(solution)/shard_map/ppermute | solution.py:403
  31.6 33.1 %all-to-all-start = ((bf16[16,96,256]{2,1,0:T(8,128)(2,1)}), bf16[16,96,256]{2,1,0:T(8,128)(2,1)S(1)}, u32[]{:S(2)}, u32[]{:S(2)}) async-start(bf16[16,96,256]{2,1,0:T(8,128)(2,1)} %pad_maximum_fusion), calls=%async_computation | async-start | bytes 1572864 | tf_op jit(solution)/shard_map/all_to_all | solution.py:409
  41.5 7.6 %collective-permute-start.4 = (bf16[144,640]{1,0:T(8,128)(2,1)S(1)}, bf16[144,640]{1,0:T(8,128)(2,1)S(1)}, u32[]{:S(2)}, u32[]{:S(2)}) collective-permute-start(bf16[144,640]{1,0:T(8,128)(2,1)S(1)} %copy-done.1), channel_id=1, source_target_pairs={{0,1},{1,2},{2,3},{3,0},{4,5},{5,6},{6,7},{7,4},{8,9},{9,10},{10,1... | collective-permute-start | bytes 552968 | tf_op jit(solution)/shard_map/ppermute | solution.py:406
  43.1 21.7 %collective-permute-start.6 = (bf16[144,640]{1,0:T(8,128)(2,1)S(1)}, bf16[144,640]{1,0:T(8,128)(2,1)S(1)}, u32[]{:S(2)}, u32[]{:S(2)}) collective-permute-start(bf16[144,640]{1,0:T(8,128)(2,1)S(1)} %copy-done.1), channel_id=1, source_target_pairs={{0,3},{1,0},{2,1},{3,2},{4,7},{5,4},{6,5},{7,6},{8,11},{9,8},{10,9... | collective-permute-start | bytes 552968 | tf_op jit(solution)/shard_map/ppermute | solution.py:408
  43.6 21.2 %collective-permute-start.5 = (bf16[144,640]{1,0:T(8,128)(2,1)S(1)}, bf16[144,640]{1,0:T(8,128)(2,1)S(1)}, u32[]{:S(2)}, u32[]{:S(2)}) collective-permute-start(bf16[144,640]{1,0:T(8,128)(2,1)S(1)} %collective-permute-done.2.refs_1_), channel_id=1, source_target_pairs={{0,1},{1,2},{2,3},{3,0},{4,5},{5,6},{6,7},{7,4},{8,9},{9,10},{10,1... | collective-permute-start | bytes 552968 | tf_op jit(solution)/shard_map/ppermute | solution.py:406
  45.1 19.7 %collective-permute-start.7 = (bf16[144,640]{1,0:T(8,128)(2,1)S(1)}, bf16[144,640]{1,0:T(8,128)(2,1)S(1)}, u32[]{:S(2)}, u32[]{:S(2)}) collective-permute-start(bf16[144,640]{1,0:T(8,128)(2,1)S(1)} %collective-permute-done.2.refs_1_), channel_id=1, source_target_pairs={{0,3},{1,0},{2,1},{3,2},{4,7},{5,4},{6,5},{7,6},{8,11},{9,8},{10,9... | collective-permute-start | bytes 552968 | tf_op jit(solution)/shard_map/ppermute | solution.py:408
  45.6 19.2 %collective-permute-start.8 = (bf16[144,640]{1,0:T(8,128)(2,1)S(1)}, bf16[144,640]{1,0:T(8,128)(2,1)}, u32[]{:S(2)}, u32[]{:S(2)}) collective-permute-start(bf16[144,640]{1,0:T(8,128)(2,1)S(1)} %copy-done.1), channel_id=1, source_target_pairs={{0,2},{1,3},{2,0},{3,1},{4,6},{5,7},{6,4},{7,5},{8,10},{9,11},{10,... | collective-permute-start | bytes 552968 | tf_op jit(solution)/shard_map/ppermute | solution.py:407
  49.1 7.1 %copy-start.3 = (bf16[144,640]{1,0:T(8,128)(2,1)}, bf16[144,640]{1,0:T(8,128)(2,1)S(1)}, u32[]{:S(2)}) copy-start(bf16[144,640]{1,0:T(8,128)(2,1)S(1)} %collective-permute-done.4.refs_2_) | copy-start | bytes 552964
  49.1 15.7 %collective-permute-start.9 = (bf16[144,640]{1,0:T(8,128)(2,1)S(1)}, bf16[144,640]{1,0:T(8,128)(2,1)}, u32[]{:S(2)}, u32[]{:S(2)}) collective-permute-start(bf16[144,640]{1,0:T(8,128)(2,1)S(1)} %collective-permute-done.2.refs_1_), channel_id=1, source_target_pairs={{0,2},{1,3},{2,0},{3,1},{4,6},{5,7},{6,4},{7,5},{8,10},{9,11},{10,... | collective-permute-start | bytes 552968 | tf_op jit(solution)/shard_map/ppermute | solution.py:407
  64.8 0.9 %copy-start = (bf16[16,96,256]{2,1,0:T(8,128)(2,1)}, bf16[16,96,256]{2,1,0:T(8,128)(2,1)S(1)}, u32[]{:S(2)}) copy-start(bf16[16,96,256]{2,1,0:T(8,128)(2,1)S(1)} %all-to-all-done.blocks_ref) | copy-start | bytes 2359300
  64.8 1.0 %copy-start.5 = (bf16[144,640]{1,0:T(8,128)(2,1)}, bf16[144,640]{1,0:T(8,128)(2,1)S(1)}, u32[]{:S(2)}) copy-start(bf16[144,640]{1,0:T(8,128)(2,1)S(1)} %collective-permute-done.5.refs_3_) | copy-start | bytes 552964
  64.8 1.0 %copy-start.4 = (bf16[144,640]{1,0:T(8,128)(2,1)}, bf16[144,640]{1,0:T(8,128)(2,1)S(1)}, u32[]{:S(2)}) copy-start(bf16[144,640]{1,0:T(8,128)(2,1)S(1)} %collective-permute-done.6.refs_4_) | copy-start | bytes 552964
  64.8 1.1 %copy-start.6 = (bf16[144,640]{1,0:T(8,128)(2,1)}, bf16[144,640]{1,0:T(8,128)(2,1)S(1)}, u32[]{:S(2)}) copy-start(bf16[144,640]{1,0:T(8,128)(2,1)S(1)} %collective-permute-done.7.refs_5_) | copy-start | bytes 552964
  72.5 13.1 %all-to-all-start.1 = ((bf16[8,64,640]{2,1,0:T(8,128)(2,1)}), bf16[8,64,640]{2,1,0:T(8,128)(2,1)S(1)}, u32[]{:S(2)}, u32[]{:S(2)}) async-start(bf16[8,64,640]{2,1,0:T(8,128)(2,1)} %shard_map.231), calls=%async_computation.1 | async-start | bytes 1310720 | tf_op jit(solution)/shard_map/all_to_all | solution.py:419

commit v5 on v4

--- a/solution.py
+++ b/solution.py
@@ -281,10 +281,11 @@
     return jnp.concatenate([upper, lower.reshape(RESP // 2, -1, mine.shape[1])], axis=1)
 
 
-def project_kernel(head_ref, blocks_ref, *refs):
-    piece_refs = refs[:8]
+def project_kernel(head_ref, blocks_hbm, *refs):
+    piece_hbm = refs[:8]
     weight_hbm = refs[8:12]
-    out_ref, weights_ref, scaled, sems = refs[12:]
+    out_ref, blocks_ref, pieces_ref, weights_ref, scaled, sems, piece_sems = refs[12:]
+    piece_refs = [pieces_ref.at[i] for i in range(8)]
     count, rows, width = out_ref.shape
     half = rows // 2
     sources = blocks_ref.shape[0]
@@ -294,8 +295,14 @@
         )
         for w, source in enumerate(weight_hbm)
     ]
-    for copy in copies:
+    blocks_copy = pltpu.make_async_copy(blocks_hbm, blocks_ref, piece_sems.at[8])
+    piece_copies = [
+        pltpu.make_async_copy(source, target, piece_sems.at[i])
+        for i, (source, target) in enumerate(zip(piece_hbm, piece_refs))
+    ]
+    for copy in [blocks_copy] + copies[:2] + piece_copies + copies[2:]:
         copy.start()
+    blocks_copy.wait()
 
     def total(first, last, part):
         summed = blocks_ref[first, part, :].astype(jnp.float32)
@@ -320,6 +327,8 @@
     inverses = []
     shrinks = []
     groups = width // 128
+    for copy in piece_copies:
+        copy.wait()
 
     def folded(values):
         return sum(values[:, g * 128 : (g + 1) * 128] for g in range(groups))
@@ -361,15 +370,18 @@
     vmem = pl.BlockSpec(memory_space=pltpu.VMEM)
     return pl.pallas_call(
         project_kernel,
-        in_specs=[SMEM] + [vmem] * 9 + [pl.BlockSpec(memory_space=pl.ANY)] * 4,
+        in_specs=[SMEM] + [pl.BlockSpec(memory_space=pl.ANY)] * 13,
         out_specs=vmem,
         out_shape=jax.ShapeDtypeStruct((HEADS, rows, width), jnp.bfloat16),
         scratch_shapes=[
+            pltpu.VMEM(blocks.shape, jnp.bfloat16),
+            pltpu.VMEM((HEADS,) + pieces[0].shape, jnp.bfloat16),
             pltpu.VMEM((2, D, 2 * HEAD), jnp.bfloat16),
             pltpu.VMEM((2, HEADS, rows, width), jnp.float32),
             pltpu.SemaphoreType.DMA((4,)),
+            pltpu.SemaphoreType.DMA((9,)),
         ],
-        compiler_params=pltpu.CompilerParams(vmem_limit_bytes=58 * 1024 * 1024),
+        compiler_params=pltpu.CompilerParams(vmem_limit_bytes=55 * 1024 * 1024),
         cost_estimate=cost(8000000, 8 * rows * D * HEAD),
     )(head, blocks, *pieces, *weights)
 

time: 86.9 us -> 86.4 us (level)
  no operation moved by 1% of the time
where the time goes in v5:
time: 86.4 us; the launch traced here: 85.8 us
  Pallas kernels  35.7 us (41%)
  starting transfers between devices  27.1 us (31%)
  waiting for transfers between devices  17 us (20%)
  other arithmetic  4.21 us (5%)
  local copies, waits for them, and re-layouts  1.08 us (1%)
    pallas_call x2, Pallas kernels, attend(): pl.pallas_call(attend_kernel, grid_spec=pltpu.PrefetchScalarGridSpec(num_...  18 us
    pallas_call x2, Pallas kernels, query_grads(): pl.pallas_call(query_kernel, grid=(pairs,), in_specs=[pl.BlockSpec((1, ro...  9.9 us
    all_to_all x1, starting transfers between devices, body(): blocks = lax.all_to_all(partial, 'resp', 0, 0, axis_index_groups=SAME_CORE)  9.85 us
    all_to_all x1, waiting for transfers between devices, body(): blocks = lax.all_to_all(partial, 'resp', 0, 0, axis_index_groups=SAME_CORE)  8.58 us
    pallas_call x1, Pallas kernels, project(): pl.pallas_call(project_kernel, in_specs=[SMEM] + [pl.BlockSpec(memory_spa...  6.15 us
    all_to_all x1, starting transfers between devices, body(): blocks = lax.all_to_all(part, 'head', 0, 0)  4.84 us
    ppermute x2, starting transfers between devices, body(): across = [lax.ppermute(one, 'head', ACROSS) for one in (own, near)]  4.25 us
    ppermute x1, starting transfers between devices, body(): from_far = lax.ppermute(sent, 'resp', FAR_SWAP)  3.28 us
  transfers between devices with their start and end apart: 12, of which 6 were waited for; matrix products, arithmetic and copies ran while one was open for 0% of the time, Pallas kernels for 24%

profile of v5, /device:TPU:2, one launch (start us, length us, event | category | flops | bytes accessed | tf_op | source)
XLA Modules:
  0.0 85.8 jit_solution(1404273073918619527)
XLA Ops:
  0.6 9.0 %shard_map.227 = (bf16[4,2176,256]{2,1,0:T(8,128)(2,1)}, bf16[128,256]{1,0:T(8,128)(2,1)}, bf16[1024,256]{1,0:T(8,128)(2,1)}, bf16[1024,256]{1,0:T(8,128)(2,1)}) custom-call(s32[1]{0:T(128)} %bitcast.core_ref, bf16[128,1024]{1,0:T(8,128)(2,1)} %q_hbm.1, bf16[128,1024]{1,0:T(8,128)(2,1)} %g_hbm.2, bf16[2048,128]{1,0:T(8,128)(2,1)} %k_ref.2, ...), custom_call_target="tpu_custom_call" | custom-call | flops 2852126720 | bytes 4194304 | tf_op jit(solution)/shard_map/pallas_call | solution.py:150
  9.7 0.1 collective-permute-start
  9.8 1.6 %shard_map.228.refs_0_ = bf16[144,640]{1,0:T(8,128)(2,1)} custom-call(bf16[64,640]{1,0:T(8,128)(2,1)} %upper_ref, bf16[64,640]{1,0:T(8,128)(2,1)} %lower_ref.1, bf16[640]{0:T(1024)(128)(2,1)} %upper_gain_ref.1, bf16[640]{0:T(1024)(128)(2,1)} %lower_gain_ref.1), custom_call_target="tpu_custom_call" | custom-call | bytes 400000 | tf_op jit(solution)/shard_map/pallas_call | solution.py:261
  11.4 0.5 collective-permute-done
  11.9 1.2 %add_convert_fusion.1 = bf16[1024,256]{1,0:T(8,128)(2,1)S(1)} fusion(bf16[1024,256]{1,0:T(8,128)(2,1)S(1)} %collective-permute-done, bf16[1024,256]{1,0:T(8,128)(2,1)} %get-tuple-element.29), kind=kLoop, calls=%fused_computation.1 | loop fusion | flops 1048576 | bytes 1572864 | tf_op jit(solution)/shard_map/convert_element_type | solution.py:271
  13.1 3.3 %collective-permute-start.1 = (bf16[16,32,256]{2,1,0:T(8,128)(2,1)S(1)}, bf16[16,32,256]{2,1,0:T(8,128)(2,1)S(1)}, u32[]{:S(2)}, u32[]{:S(2)}) collective-permute-start(bf16[16,32,256]{2,1,0:T(8,128)(2,1)S(1)} %select_bitcast_fusion), channel_id=1, source_target_pairs={{0,128},{8,136},{16,144},{24,152},{32,160},{40,168},{48,176},{56,1... | collective-permute-start | bytes 786440 | tf_op jit(solution)/shard_map/ppermute | solution.py:408
  16.4 0.7 collective-permute-start.2
  17.1 8.9 %shard_map.229 = (bf16[4,2176,256]{2,1,0:T(8,128)(2,1)}, bf16[128,256]{1,0:T(8,128)(2,1)}, bf16[1024,256]{1,0:T(8,128)(2,1)}, bf16[1024,256]{1,0:T(8,128)(2,1)}) custom-call(s32[1]{0:T(128)} %bitcast.core_ref, bf16[128,1024]{1,0:T(8,128)(2,1)} %q_hbm.2, bf16[128,1024]{1,0:T(8,128)(2,1)} %g_hbm.3, bf16[2048,128]{1,0:T(8,128)(2,1)} %k_ref.3, ...), custom_call_target="tpu_custom_call" | custom-call | flops 2852126720 | bytes 4194304 | tf_op jit(solution)/shard_map/pallas_call | solution.py:150
  26.1 1.3 %collective-permute-done.2.refs_1_ = bf16[144,640]{1,0:T(8,128)(2,1)S(1)} collective-permute-done((bf16[144,640]{1,0:T(8,128)(2,1)S(1)}, bf16[144,640]{1,0:T(8,128)(2,1)S(1)}, u32[]{:S(2)}, u32[]{:S(2)}) %collective-permute-start.2) | collective-permute-done | bytes 184352 | tf_op jit(solution)/shard_map/ppermute | solution.py:409
  27.4 0.1 fusion
  27.5 2.0 %collective-permute-done.3 = bf16[1024,256]{1,0:T(8,128)(2,1)S(1)} collective-permute-done((bf16[1024,256]{1,0:T(8,128)(2,1)}, bf16[1024,256]{1,0:T(8,128)(2,1)S(1)}, u32[]{:S(2)}, u32[]{:S(2)}) %collective-permute-start.3) | collective-permute-done | bytes 524320 | tf_op jit(solution)/shard_map/ppermute | solution.py:415
  29.5 1.2 %add_convert_fusion = bf16[1024,256]{1,0:T(8,128)(2,1)S(1)} fusion(bf16[1024,256]{1,0:T(8,128)(2,1)S(1)} %collective-permute-done.3, bf16[1024,256]{1,0:T(8,128)(2,1)} %get-tuple-element.38), kind=kLoop, calls=%fused_computation | loop fusion | flops 1048576 | bytes 1572864 | tf_op jit(solution)/shard_map/convert_element_type | solution.py:280
  30.7 1.0 %pad_maximum_fusion = bf16[16,96,256]{2,1,0:T(8,128)(2,1)} fusion(bf16[16,64,256]{2,1,0:T(8,128)(2,1)S(1)} %bitcast.23, bf16[16,32,256]{2,1,0:T(8,128)(2,1)S(1)} %fusion), kind=kLoop, calls=%fused_computation.2 | loop fusion | flops 1572864 | bytes 1572864 | tf_op jit(solution)/shard_map/concatenate | solution.py:281
  31.6 9.8 %all-to-all-start = ((bf16[16,96,256]{2,1,0:T(8,128)(2,1)}), bf16[16,96,256]{2,1,0:T(8,128)(2,1)S(1)}, u32[]{:S(2)}, u32[]{:S(2)}) async-start(bf16[16,96,256]{2,1,0:T(8,128)(2,1)} %pad_maximum_fusion), calls=%async_computation | async-start | bytes 1572864 | tf_op jit(solution)/shard_map/all_to_all | solution.py:421
  41.5 1.6 %collective-permute-start.4 = (bf16[144,640]{1,0:T(8,128)(2,1)S(1)}, bf16[144,640]{1,0:T(8,128)(2,1)S(1)}, u32[]{:S(2)}, u32[]{:S(2)}) collective-permute-start(bf16[144,640]{1,0:T(8,128)(2,1)S(1)} %copy-done.1), channel_id=1, source_target_pairs={{0,1},{1,2},{2,3},{3,0},{4,5},{5,6},{6,7},{7,4},{8,9},{9,10},{10,1... | collective-permute-start | bytes 552968 | tf_op jit(solution)/shard_map/ppermute | solution.py:418
  43.1 0.5 collective-permute-start.6
  43.6 1.5 %collective-permute-start.5 = (bf16[144,640]{1,0:T(8,128)(2,1)S(1)}, bf16[144,640]{1,0:T(8,128)(2,1)S(1)}, u32[]{:S(2)}, u32[]{:S(2)}) collective-permute-start(bf16[144,640]{1,0:T(8,128)(2,1)S(1)} %collective-permute-done.2.refs_1_), channel_id=1, source_target_pairs={{0,1},{1,2},{2,3},{3,0},{4,5},{5,6},{6,7},{7,4},{8,9},{9,10},{10,1... | collective-permute-start | bytes 552968 | tf_op jit(solution)/shard_map/ppermute | solution.py:418
  45.1 0.5 collective-permute-start.7
  45.6 2.1 %collective-permute-start.8 = (bf16[144,640]{1,0:T(8,128)(2,1)S(1)}, bf16[144,640]{1,0:T(8,128)(2,1)}, u32[]{:S(2)}, u32[]{:S(2)}) collective-permute-start(bf16[144,640]{1,0:T(8,128)(2,1)S(1)} %copy-done.1), channel_id=1, source_target_pairs={{0,2},{1,3},{2,0},{3,1},{4,6},{5,7},{6,4},{7,5},{8,10},{9,11},{10,... | collective-permute-start | bytes 552968 | tf_op jit(solution)/shard_map/ppermute | solution.py:419
  47.7 1.3 %collective-permute-done.4.refs_2_ = bf16[144,640]{1,0:T(8,128)(2,1)S(1)} collective-permute-done((bf16[144,640]{1,0:T(8,128)(2,1)S(1)}, bf16[144,640]{1,0:T(8,128)(2,1)S(1)}, u32[]{:S(2)}, u32[]{:S(2)}) %collective-permute-start.4) | collective-permute-done | bytes 184352 | tf_op jit(solution)/shard_map/ppermute | solution.py:418
  49.1 2.1 %collective-permute-start.9 = (bf16[144,640]{1,0:T(8,128)(2,1)S(1)}, bf16[144,640]{1,0:T(8,128)(2,1)}, u32[]{:S(2)}, u32[]{:S(2)}) collective-permute-start(bf16[144,640]{1,0:T(8,128)(2,1)S(1)} %collective-permute-done.2.refs_1_), channel_id=1, source_target_pairs={{0,2},{1,3},{2,0},{3,1},{4,6},{5,7},{6,4},{7,5},{8,10},{9,11},{10,... | collective-permute-start | bytes 552968 | tf_op jit(solution)/shard_map/ppermute | solution.py:419
  51.2 4.9 %shard_map.230 = bf16[128,1024]{1,0:T(8,128)(2,1)} custom-call(bf16[4,2176,256]{2,1,0:T(8,128)(2,1)} %get-tuple-element.43.slopes_ref, bf16[2048,128]{1,0:T(8,128)(2,1)} %k_ref.2, bf16[128,128]{1,0:T(8,128)(2,1)} %sk_ref.2), custom_call_target="tpu_custom_call" | custom-call | flops 570425344 | bytes 6291456 | tf_op jit(solution)/shard_map/pallas_call | solution.py:209
  56.2 8.6 %all-to-all-done.blocks_hbm = bf16[16,96,256]{2,1,0:T(8,128)(2,1)S(1)} async-done(((bf16[16,96,256]{2,1,0:T(8,128)(2,1)}), bf16[16,96,256]{2,1,0:T(8,128)(2,1)S(1)}, u32[]{:S(2)}, u32[]{:S(2)}) %all-to-all-start) | async-done | bytes 786464 | tf_op jit(solution)/shard_map/all_to_all | solution.py:421
  64.8 0.8 copy-done
  65.6 0.1 copy-done.5
  65.7 0.1 copy-done.4
  65.8 0.1 copy-done.6
  65.9 6.1 %shard_map.231 = bf16[8,64,640]{2,1,0:T(8,128)(2,1)} custom-call(s32[1]{0:T(128)} %bitcast.5.head_ref, bf16[16,96,256]{2,1,0:T(8,128)(2,1)} %copy-done, bf16[144,640]{1,0:T(8,128)(2,1)} %shard_map.228.refs_0_, bf16[144,640]{1,0:T(8,128)(2,1)} %copy-done.2, bf16[144,640]{1,0:T(8,128)(2,1)} %copy-done.3, bf16[144,640]{1,0:T(8,128)(2,1)} %copy-done.5, ...), custom_call_target="tpu_custom_call" | custom-call | flops 335544320 | bytes 8000000 | tf_op jit(solution)/shard_map/pallas_call | solution.py:371
  72.0 4.8 %all-to-all-start.1 = ((bf16[8,64,640]{2,1,0:T(8,128)(2,1)}), bf16[8,64,640]{2,1,0:T(8,128)(2,1)S(1)}, u32[]{:S(2)}, u32[]{:S(2)}) async-start(bf16[8,64,640]{2,1,0:T(8,128)(2,1)} %shard_map.231), calls=%async_computation.1 | async-start | bytes 1310720 | tf_op jit(solution)/shard_map/all_to_all | solution.py:431
  76.9 4.9 %shard_map.232 = bf16[128,1024]{1,0:T(8,128)(2,1)} custom-call(bf16[4,2176,256]{2,1,0:T(8,128)(2,1)} %get-tuple-element.49.slopes_ref, bf16[2048,128]{1,0:T(8,128)(2,1)} %k_ref.3, bf16[128,128]{1,0:T(8,128)(2,1)} %sk_ref.3), custom_call_target="tpu_custom_call" | custom-call | flops 570425344 | bytes 6291456 | tf_op jit(solution)/shard_map/pallas_call | solution.py:209
  81.8 3.3 %all-to-all-done.1 = bf16[8,64,640]{2,1,0:T(8,128)(2,1)S(1)} async-done(((bf16[8,64,640]{2,1,0:T(8,128)(2,1)}), bf16[8,64,640]{2,1,0:T(8,128)(2,1)S(1)}, u32[]{:S(2)}, u32[]{:S(2)}) %all-to-all-start.1) | async-done | bytes 655392 | tf_op jit(solution)/shard_map/all_to_all | solution.py:431
  85.1 0.7 reduce_sum.12
  (18 shorter events, 0.1 us)
Async XLA Ops:
  9.7 2.2 %collective-permute-start = (bf16[1024,256]{1,0:T(8,128)(2,1)}, bf16[1024,256]{1,0:T(8,128)(2,1)S(1)}, u32[]{:S(2)}, u32[]{:S(2)}) collective-permute-start(bf16[1024,256]{1,0:T(8,128)(2,1)} %get-tuple-element.31), channel_id=1, source_target_pairs={{0,8},{8,0},{16,24},{24,16},{32,40},{40,32},{48,56},{56,48},{64,72... | collective-permute-start | bytes 1572872 | tf_op jit(solution)/shard_map/ppermute | solution.py:404
  11.4 5.0 %copy-start.1 = (bf16[144,640]{1,0:T(8,128)(2,1)S(1)}, bf16[144,640]{1,0:T(8,128)(2,1)}, u32[]{:S(2)}) copy-start(bf16[144,640]{1,0:T(8,128)(2,1)} %shard_map.228.refs_0_) | copy-start | bytes 552964
  13.1 14.2 %collective-permute-start.1 = (bf16[16,32,256]{2,1,0:T(8,128)(2,1)S(1)}, bf16[16,32,256]{2,1,0:T(8,128)(2,1)S(1)}, u32[]{:S(2)}, u32[]{:S(2)}) collective-permute-start(bf16[16,32,256]{2,1,0:T(8,128)(2,1)S(1)} %select_bitcast_fusion), channel_id=1, source_target_pairs={{0,128},{8,136},{16,144},{24,152},{32,160},{40,168},{48,176},{56,1... | collective-permute-start | bytes 786440 | tf_op jit(solution)/shard_map/ppermute | solution.py:408
  16.4 10.9 %collective-permute-start.2 = (bf16[144,640]{1,0:T(8,128)(2,1)S(1)}, bf16[144,640]{1,0:T(8,128)(2,1)S(1)}, u32[]{:S(2)}, u32[]{:S(2)}) collective-permute-start(bf16[144,640]{1,0:T(8,128)(2,1)S(1)} %copy-done.1), channel_id=1, source_target_pairs={{0,4},{1,5},{2,6},{3,7},{4,0},{5,1},{6,2},{7,3},{8,12},{9,13},{10,... | collective-permute-start | bytes 552968 | tf_op jit(solution)/shard_map/ppermute | solution.py:409
  27.4 21.7 %copy-start.2 = (bf16[144,640]{1,0:T(8,128)(2,1)}, bf16[144,640]{1,0:T(8,128)(2,1)S(1)}, u32[]{:S(2)}) copy-start(bf16[144,640]{1,0:T(8,128)(2,1)S(1)} %collective-permute-done.2.refs_1_) | copy-start | bytes 552964
  27.4 2.1 %collective-permute-start.3 = (bf16[1024,256]{1,0:T(8,128)(2,1)}, bf16[1024,256]{1,0:T(8,128)(2,1)S(1)}, u32[]{:S(2)}, u32[]{:S(2)}) collective-permute-start(bf16[1024,256]{1,0:T(8,128)(2,1)} %get-tuple-element.39), channel_id=1, source_target_pairs={{0,8},{8,0},{16,24},{24,16},{32,40},{40,32},{48,56},{56,48},{64,72... | collective-permute-start | bytes 1572872 | tf_op jit(solution)/shard_map/ppermute | solution.py:415
  31.6 33.1 %all-to-all-start = ((bf16[16,96,256]{2,1,0:T(8,128)(2,1)}), bf16[16,96,256]{2,1,0:T(8,128)(2,1)S(1)}, u32[]{:S(2)}, u32[]{:S(2)}) async-start(bf16[16,96,256]{2,1,0:T(8,128)(2,1)} %pad_maximum_fusion), calls=%async_computation | async-start | bytes 1572864 | tf_op jit(solution)/shard_map/all_to_all | solution.py:421
  41.5 7.6 %collective-permute-start.4 = (bf16[144,640]{1,0:T(8,128)(2,1)S(1)}, bf16[144,640]{1,0:T(8,128)(2,1)S(1)}, u32[]{:S(2)}, u32[]{:S(2)}) collective-permute-start(bf16[144,640]{1,0:T(8,128)(2,1)S(1)} %copy-done.1), channel_id=1, source_target_pairs={{0,1},{1,2},{2,3},{3,0},{4,5},{5,6},{6,7},{7,4},{8,9},{9,10},{10,1... | collective-permute-start | bytes 552968 | tf_op jit(solution)/shard_map/ppermute | solution.py:418
  43.1 21.7 %collective-permute-start.6 = (bf16[144,640]{1,0:T(8,128)(2,1)S(1)}, bf16[144,640]{1,0:T(8,128)(2,1)S(1)}, u32[]{:S(2)}, u32[]{:S(2)}) collective-permute-start(bf16[144,640]{1,0:T(8,128)(2,1)S(1)} %copy-done.1), channel_id=1, source_target_pairs={{0,3},{1,0},{2,1},{3,2},{4,7},{5,4},{6,5},{7,6},{8,11},{9,8},{10,9... | collective-permute-start | bytes 552968 | tf_op jit(solution)/shard_map/ppermute | solution.py:420
  43.6 21.2 %collective-permute-start.5 = (bf16[144,640]{1,0:T(8,128)(2,1)S(1)}, bf16[144,640]{1,0:T(8,128)(2,1)S(1)}, u32[]{:S(2)}, u32[]{:S(2)}) collective-permute-start(bf16[144,640]{1,0:T(8,128)(2,1)S(1)} %collective-permute-done.2.refs_1_), channel_id=1, source_target_pairs={{0,1},{1,2},{2,3},{3,0},{4,5},{5,6},{6,7},{7,4},{8,9},{9,10},{10,1... | collective-permute-start | bytes 552968 | tf_op jit(solution)/shard_map/ppermute | solution.py:418
  45.1 19.7 %collective-permute-start.7 = (bf16[144,640]{1,0:T(8,128)(2,1)S(1)}, bf16[144,640]{1,0:T(8,128)(2,1)S(1)}, u32[]{:S(2)}, u32[]{:S(2)}) collective-permute-start(bf16[144,640]{1,0:T(8,128)(2,1)S(1)} %collective-permute-done.2.refs_1_), channel_id=1, source_target_pairs={{0,3},{1,0},{2,1},{3,2},{4,7},{5,4},{6,5},{7,6},{8,11},{9,8},{10,9... | collective-permute-start | bytes 552968 | tf_op jit(solution)/shard_map/ppermute | solution.py:420
  45.6 19.2 %collective-permute-start.8 = (bf16[144,640]{1,0:T(8,128)(2,1)S(1)}, bf16[144,640]{1,0:T(8,128)(2,1)}, u32[]{:S(2)}, u32[]{:S(2)}) collective-permute-start(bf16[144,640]{1,0:T(8,128)(2,1)S(1)} %copy-done.1), channel_id=1, source_target_pairs={{0,2},{1,3},{2,0},{3,1},{4,6},{5,7},{6,4},{7,5},{8,10},{9,11},{10,... | collective-permute-start | bytes 552968 | tf_op jit(solution)/shard_map/ppermute | solution.py:419
  49.1 7.1 %copy-start.3 = (bf16[144,640]{1,0:T(8,128)(2,1)}, bf16[144,640]{1,0:T(8,128)(2,1)S(1)}, u32[]{:S(2)}) copy-start(bf16[144,640]{1,0:T(8,128)(2,1)S(1)} %collective-permute-done.4.refs_2_) | copy-start | bytes 552964
  49.1 15.7 %collective-permute-start.9 = (bf16[144,640]{1,0:T(8,128)(2,1)S(1)}, bf16[144,640]{1,0:T(8,128)(2,1)}, u32[]{:S(2)}, u32[]{:S(2)}) collective-permute-start(bf16[144,640]{1,0:T(8,128)(2,1)S(1)} %collective-permute-done.2.refs_1_), channel_id=1, source_target_pairs={{0,2},{1,3},{2,0},{3,1},{4,6},{5,7},{6,4},{7,5},{8,10},{9,11},{10,... | collective-permute-start | bytes 552968 | tf_op jit(solution)/shard_map/ppermute | solution.py:419
  64.8 0.9 %copy-start = (bf16[16,96,256]{2,1,0:T(8,128)(2,1)}, bf16[16,96,256]{2,1,0:T(8,128)(2,1)S(1)}, u32[]{:S(2)}) copy-start(bf16[16,96,256]{2,1,0:T(8,128)(2,1)S(1)} %all-to-all-done.blocks_hbm) | copy-start | bytes 2359300
  64.8 1.0 %copy-start.5 = (bf16[144,640]{1,0:T(8,128)(2,1)}, bf16[144,640]{1,0:T(8,128)(2,1)S(1)}, u32[]{:S(2)}) copy-start(bf16[144,640]{1,0:T(8,128)(2,1)S(1)} %collective-permute-done.5.refs_3_) | copy-start | bytes 552964
  64.8 1.0 %copy-start.4 = (bf16[144,640]{1,0:T(8,128)(2,1)}, bf16[144,640]{1,0:T(8,128)(2,1)S(1)}, u32[]{:S(2)}) copy-start(bf16[144,640]{1,0:T(8,128)(2,1)S(1)} %collective-permute-done.6.refs_4_) | copy-start | bytes 552964
  64.8 1.1 %copy-start.6 = (bf16[144,640]{1,0:T(8,128)(2,1)}, bf16[144,640]{1,0:T(8,128)(2,1)S(1)}, u32[]{:S(2)}) copy-start(bf16[144,640]{1,0:T(8,128)(2,1)S(1)} %collective-permute-done.7.refs_5_) | copy-start | bytes 552964
  72.0 13.1 %all-to-all-start.1 = ((bf16[8,64,640]{2,1,0:T(8,128)(2,1)}), bf16[8,64,640]{2,1,0:T(8,128)(2,1)S(1)}, u32[]{:S(2)}, u32[]{:S(2)}) async-start(bf16[8,64,640]{2,1,0:T(8,128)(2,1)} %shard_map.231), calls=%async_computation.1 | async-start | bytes 1310720 | tf_op jit(solution)/shard_map/all_to_all | solution.py:431
